TPU v7x, 128 devices: a whole 4x4x4 slice. The times are simulated.
128 devices in a mesh: dp: 128 (over y, z, x, core).
Axes of the slice: x: 4, y: 4, z: 4, core: 2. Of those that a mesh axis runs over, the one named last changes fastest.
Arguments:
- images: bfloat16 [98304, 1152], P('dp'), may hold values from -0.19921875 to 0.19921875
- texts: bfloat16 [98304, 1152], P('dp'), may hold values from -0.19921875 to 0.19921875
- pair_ids: int32 [98304], P('dp'), may hold values from 0 to 191
- log_scale: float32 [1], replicated, may hold values from 1 to 2.3
- bias: float32 [1], replicated, may hold values from -6 to -2
Outputs:
- grad_images: float32 [98304, 1152], P('dp')
- grad_texts: float32 [98304, 1152], P('dp')
All inputs are finite; a program needn't handle non-finite values.
Results may differ from a plain program's by a relative error of at most 0.0042.
Values may be sent and summed in bfloat16 or wider, within the bound.
No kernel may reach another device: no remote copies, remote signals or barrier semaphores. Data moves between devices by JAX's collectives and lax.ppermute only.
A program may use at most 128 MiB of HBM per device.

v0:
```python
import jax
import jax.numpy as jnp
from jax import lax
from jax.sharding import PartitionSpec as P

STEPS = 4


def shifted(value, axis, steps):
    count = lax.axis_size(axis)
    pairs = [(source, (source + steps) % count) for source in range(count)]
    return lax.ppermute(value, axis, pairs)


def unit(rows):
    rows32 = rows.astype(jnp.float32)
    norms = jnp.sqrt(jnp.sum(rows32 * rows32, axis=1, keepdims=True) + 1e-06)
    return (rows32 / norms, norms)


def weights(image_block, text_block, image_labels, text_labels, log_scale, bias):
    scale = jnp.exp(log_scale[0])
    logits = (
        scale
        * lax.dot_general(
            image_block, text_block, (((1,), (1,)), ((), ())), preferred_element_type=jnp.float32
        )
        + bias[0]
    )
    signs = jnp.where(image_labels[:, None] == text_labels[None, :], 1.0, -1.0).astype(jnp.float32)
    return (scale * -signs * jax.nn.sigmoid(-signs * logits)).astype(jnp.bfloat16)


def back_through(exact, norms, grad):
    return (grad - exact * jnp.sum(exact * grad, axis=1, keepdims=True)) / norms


def on_device(images, texts, pair_ids, log_scale, bias):
    image_exact, image_norms = unit(images)
    image_unit = image_exact.astype(jnp.bfloat16)
    text_exact, text_norms = unit(texts)
    text_unit = text_exact.astype(jnp.bfloat16)
    visiting = text_unit
    visiting_ids = pair_ids
    grad_image = jnp.zeros(image_exact.shape, jnp.float32)
    own_grad = jnp.zeros(text_exact.shape, jnp.float32)
    running = own_grad
    for offset in range(STEPS):
        if offset > 0:
            visiting, visiting_ids = shifted((visiting, visiting_ids), "dp", -1)
        coef = weights(image_unit, visiting, pair_ids, visiting_ids, log_scale, bias)
        grad_image = grad_image + jnp.dot(coef, visiting, preferred_element_type=jnp.float32)
        partial_grad = lax.dot_general(
            coef, image_unit, (((0,), (0,)), ((), ())), preferred_element_type=jnp.float32
        )
        if offset == 0:
            running = partial_grad
        else:
            running = shifted(running, "dp", -1) + partial_grad
    own_grad = shifted(running, "dp", STEPS - 1)
    return (
        back_through(image_exact, image_norms, grad_image),
        back_through(text_exact, text_norms, own_grad),
    )


def solution(mesh):
    in_specs = (P("dp", None), P("dp", None), P("dp"), P(), P())
    out_specs = (P("dp", None), P("dp", None))
    return jax.shard_map(
        on_device, mesh=mesh, in_specs=in_specs, out_specs=out_specs, check_vma=False
    )
```

profile of v0, /device:TPU:0, one launch (start us, length us, event | category | flops | bytes accessed | tf_op | source)
XLA Modules:
  0.0 343.8 jit_solution(10426085228101453161)
XLA Ops:
  0.6 0.0 copy-start.1
  0.6 0.0 copy-start
  0.6 2.0 fusion
  2.7 0.0 copy-done.1
  2.7 0.6 fusion.2
  3.3 0.0 copy-done
  3.3 0.0 copy-start.2
  3.3 0.4 fusion.1
  3.7 0.6 fusion.3
  5.7 0.0 copy-done.2
  5.7 2.2 multiply_convert_fusion.3
  7.9 1.8 fusion.5
  9.6 8.3 %collective-permute-start.6 = (f32[768,1152]{1,0:T(8,128)S(1)}, f32[768,1152]{1,0:T(8,128)S(1)}, u32[]{:S(2)}, u32[]{:S(2)}) collective-permute-start(f32[768,1152]{1,0:T(8,128)S(1)} %fusion.5), channel_id=1, source_target_pairs={{0,127},{1,0},{2,1},{3,2},{4,3},{5,4},{6,5},{7,6},{8,7},{9,8},{10,... | collective-permute-start | bytes 10616840 | tf_op jit(solution)/shard_map/ppermute | solution.py:12
  17.9 0.7 collective-permute-start.1
  18.6 0.3 collective-permute-start
  18.9 57.1 %collective-permute-done = s32[768]{0:T(1024)S(1)} collective-permute-done((s32[768]{0:T(1024)S(1)}, s32[768]{0:T(1024)S(1)}, u32[]{:S(2)}, u32[]{:S(2)}) %collective-permute-start) | collective-permute-done | bytes 3104 | tf_op jit(solution)/shard_map/ppermute | solution.py:12
  75.9 0.0 collective-permute-done.1
  75.9 2.2 multiply_convert_fusion.2
  78.2 0.0 collective-permute-done.6
  78.2 1.9 convolution_add_fusion
  80.1 7.4 %collective-permute-start.7 = (f32[768,1152]{1,0:T(8,128)S(1)}, f32[768,1152]{1,0:T(8,128)S(1)}, u32[]{:S(2)}, u32[]{:S(2)}) collective-permute-start(f32[768,1152]{1,0:T(8,128)S(1)} %convolution_add_fusion), channel_id=1, source_target_pairs={{0,127},{1,0},{2,1},{3,2},{4,3},{5,4},{6,5},{7,6},{8,7},{9,8},{10,... | collective-permute-start | bytes 10616840 | tf_op jit(solution)/shard_map/ppermute | solution.py:12
  87.5 0.1 collective-permute-start.3
  87.5 0.3 collective-permute-start.2
  87.8 57.7 %collective-permute-done.2 = s32[768]{0:T(1024)S(1)} collective-permute-done((s32[768]{0:T(1024)S(1)}, s32[768]{0:T(1024)S(1)}, u32[]{:S(2)}, u32[]{:S(2)}) %collective-permute-start.2) | collective-permute-done | bytes 3104 | tf_op jit(solution)/shard_map/ppermute | solution.py:12
  145.5 0.0 collective-permute-done.3
  145.5 2.2 multiply_convert_fusion.1
  147.7 1.8 fusion.6
  149.5 0.0 collective-permute-done.7
  149.5 0.4 add.79
  149.9 7.4 %collective-permute-start.8 = (f32[768,1152]{1,0:T(8,128)S(1)}, f32[768,1152]{1,0:T(8,128)S(1)}, u32[]{:S(2)}, u32[]{:S(2)}) collective-permute-start(f32[768,1152]{1,0:T(8,128)S(1)} %add.79), channel_id=1, source_target_pairs={{0,127},{1,0},{2,1},{3,2},{4,3},{5,4},{6,5},{7,6},{8,7},{9,8},{10,... | collective-permute-start | bytes 10616840 | tf_op jit(solution)/shard_map/ppermute | solution.py:12
  157.3 0.1 collective-permute-start.5
  157.3 0.1 collective-permute-start.4
  157.4 95.8 %collective-permute-done.4 = s32[768]{0:T(1024)S(1)} collective-permute-done((s32[768]{0:T(1024)S(1)}, s32[768]{0:T(1024)S(1)}, u32[]{:S(2)}, u32[]{:S(2)}) %collective-permute-start.4) | collective-permute-done | bytes 3104 | tf_op jit(solution)/shard_map/ppermute | solution.py:12
  253.2 0.0 collective-permute-done.5
  253.2 2.2 multiply_convert_fusion
  255.4 1.8 fusion.7
  257.2 0.0 collective-permute-done.8
  257.2 0.4 add.80
  257.6 0.3 collective-permute-start.9
  257.9 1.7 fusion.4
  259.6 1.8 convolution_add_fusion.3
  261.4 1.8 convolution_add_fusion.2
  263.2 2.0 multiply_reduce_fusion.1
  265.1 2.5 subtract_divide_fusion.1
  267.6 73.1 %collective-permute-done.9 = f32[768,1152]{1,0:T(8,128)S(1)} collective-permute-done((f32[768,1152]{1,0:T(8,128)S(1)}, f32[768,1152]{1,0:T(8,128)S(1)}, u32[]{:S(2)}, u32[]{:S(2)}) %collective-permute-start.9) | collective-permute-done | bytes 3538976 | tf_op jit(solution)/shard_map/ppermute | solution.py:12
  340.7 0.6 multiply_reduce_fusion
  341.4 2.5 subtract_divide_fusion
  (2 shorter events, 0.0 us)
Async XLA Ops:
  0.6 2.1 copy-start.1
  0.6 2.7 copy-start
  3.3 2.4 copy-start.2
  9.6 68.5 %collective-permute-start.6 = (f32[768,1152]{1,0:T(8,128)S(1)}, f32[768,1152]{1,0:T(8,128)S(1)}, u32[]{:S(2)}, u32[]{:S(2)}) collective-permute-start(f32[768,1152]{1,0:T(8,128)S(1)} %fusion.5), channel_id=1, source_target_pairs={{0,127},{1,0},{2,1},{3,2},{4,3},{5,4},{6,5},{7,6},{8,7},{9,8},{10,... | collective-permute-start | bytes 10616840 | tf_op jit(solution)/shard_map/ppermute | solution.py:12
  17.9 58.0 %collective-permute-start.1 = (bf16[768,1152]{1,0:T(8,128)(2,1)S(1)}, bf16[768,1152]{1,0:T(8,128)(2,1)S(1)}, u32[]{:S(2)}, u32[]{:S(2)}) collective-permute-start(bf16[768,1152]{1,0:T(8,128)(2,1)S(1)} %fusion.3), channel_id=1, source_target_pairs={{0,127},{1,0},{2,1},{3,2},{4,3},{5,4},{6,5},{7,6},{8,7},{9,8},{10,... | collective-permute-start | bytes 5308424 | tf_op jit(solution)/shard_map/ppermute | solution.py:12
  18.6 57.3 %collective-permute-start = (s32[768]{0:T(1024)S(1)}, s32[768]{0:T(1024)S(1)}, u32[]{:S(2)}, u32[]{:S(2)}) collective-permute-start(s32[768]{0:T(1024)S(1)} %copy-done.2), channel_id=1, source_target_pairs={{0,127},{1,0},{2,1},{3,2},{4,3},{5,4},{6,5},{7,6},{8,7},{9,8},{10,... | collective-permute-start | bytes 9224 | tf_op jit(solution)/shard_map/ppermute | solution.py:12
  80.1 69.4 %collective-permute-start.7 = (f32[768,1152]{1,0:T(8,128)S(1)}, f32[768,1152]{1,0:T(8,128)S(1)}, u32[]{:S(2)}, u32[]{:S(2)}) collective-permute-start(f32[768,1152]{1,0:T(8,128)S(1)} %convolution_add_fusion), channel_id=1, source_target_pairs={{0,127},{1,0},{2,1},{3,2},{4,3},{5,4},{6,5},{7,6},{8,7},{9,8},{10,... | collective-permute-start | bytes 10616840 | tf_op jit(solution)/shard_map/ppermute | solution.py:12
  87.5 58.0 %collective-permute-start.3 = (bf16[768,1152]{1,0:T(8,128)(2,1)S(1)}, bf16[768,1152]{1,0:T(8,128)(2,1)S(1)}, u32[]{:S(2)}, u32[]{:S(2)}) collective-permute-start(bf16[768,1152]{1,0:T(8,128)(2,1)S(1)} %collective-permute-done.1), channel_id=1, source_target_pairs={{0,127},{1,0},{2,1},{3,2},{4,3},{5,4},{6,5},{7,6},{8,7},{9,8},{10,... | collective-permute-start | bytes 5308424 | tf_op jit(solution)/shard_map/ppermute | solution.py:12
  87.5 57.9 %collective-permute-start.2 = (s32[768]{0:T(1024)S(1)}, s32[768]{0:T(1024)S(1)}, u32[]{:S(2)}, u32[]{:S(2)}) collective-permute-start(s32[768]{0:T(1024)S(1)} %collective-permute-done), channel_id=1, source_target_pairs={{0,127},{1,0},{2,1},{3,2},{4,3},{5,4},{6,5},{7,6},{8,7},{9,8},{10,... | collective-permute-start | bytes 9224 | tf_op jit(solution)/shard_map/ppermute | solution.py:12
  149.9 107.3 %collective-permute-start.8 = (f32[768,1152]{1,0:T(8,128)S(1)}, f32[768,1152]{1,0:T(8,128)S(1)}, u32[]{:S(2)}, u32[]{:S(2)}) collective-permute-start(f32[768,1152]{1,0:T(8,128)S(1)} %add.79), channel_id=1, source_target_pairs={{0,127},{1,0},{2,1},{3,2},{4,3},{5,4},{6,5},{7,6},{8,7},{9,8},{10,... | collective-permute-start | bytes 10616840 | tf_op jit(solution)/shard_map/ppermute | solution.py:12
  157.3 95.9 %collective-permute-start.5 = (bf16[768,1152]{1,0:T(8,128)(2,1)S(1)}, bf16[768,1152]{1,0:T(8,128)(2,1)S(1)}, u32[]{:S(2)}, u32[]{:S(2)}) collective-permute-start(bf16[768,1152]{1,0:T(8,128)(2,1)S(1)} %collective-permute-done.3), channel_id=1, source_target_pairs={{0,127},{1,0},{2,1},{3,2},{4,3},{5,4},{6,5},{7,6},{8,7},{9,8},{10,... | collective-permute-start | bytes 5308424 | tf_op jit(solution)/shard_map/ppermute | solution.py:12
  157.3 95.8 %collective-permute-start.4 = (s32[768]{0:T(1024)S(1)}, s32[768]{0:T(1024)S(1)}, u32[]{:S(2)}, u32[]{:S(2)}) collective-permute-start(s32[768]{0:T(1024)S(1)} %collective-permute-done.2), channel_id=1, source_target_pairs={{0,127},{1,0},{2,1},{3,2},{4,3},{5,4},{6,5},{7,6},{8,7},{9,8},{10,... | collective-permute-start | bytes 9224 | tf_op jit(solution)/shard_map/ppermute | solution.py:12
  257.6 83.2 %collective-permute-start.9 = (f32[768,1152]{1,0:T(8,128)S(1)}, f32[768,1152]{1,0:T(8,128)S(1)}, u32[]{:S(2)}, u32[]{:S(2)}) collective-permute-start(f32[768,1152]{1,0:T(8,128)S(1)} %add.80), channel_id=1, source_target_pairs={{0,3},{1,4},{2,5},{3,6},{4,7},{5,8},{6,9},{7,10},{8,11},{9,12},{10... | collective-permute-start | bytes 10616840 | tf_op jit(solution)/shard_map/ppermute | solution.py:12
where the time goes:
time: 344 us
  waiting for transfers between devices  284 us (83%)
  starting transfers between devices  24.8 us (7%)
  matrix products  23.3 us (7%)
  other arithmetic  9.87 us (3%)
    ppermute x10, waiting for transfers between devices, shifted(): return lax.ppermute(value, axis, pairs)  284 us
    ppermute x10, starting transfers between devices, shifted(): return lax.ppermute(value, axis, pairs)  24.8 us
    dot_general x4, matrix products, weights(): lax.dot_general(image_block, text_block, (((1,), (1,)), ((), ())), prefer...  8.95 us
    dot_general x4, matrix products, on_device(): jnp.dot(coef, visiting, preferred_element_type=jnp.float32)  7.24 us
    dot_general x4, matrix products, on_device(): lax.dot_general(coef, image_unit, (((0,), (0,)), ((), ())), preferred_ele...  7.13 us
  transfers between devices with their start and end apart: 10, of which 4 were waited for; matrix products, arithmetic and copies ran while one was open for 6% of the time, Pallas kernels for 0%

commit v1 on v0

v1 whole, which is shorter than its diff:
```python
import functools

import jax
import jax.numpy as jnp
from jax import lax
from jax.experimental import pallas as pl
from jax.experimental.pallas import tpu as pltpu
from jax.sharding import PartitionSpec as P

AXIS = "dp"
TILE = 256
PIECES = (384, 256, 128)
LIMIT = 24 * 1024 * 1024
HBM = pl.BlockSpec(memory_space=pl.ANY)
SMEM = pl.BlockSpec(memory_space=pltpu.SMEM)


def is_even():
    return lax.rem(lax.axis_index(AXIS), 2) == 0


def call(kernel, **kw):
    return pl.pallas_call(
        kernel, compiler_params=pltpu.CompilerParams(vmem_limit_bytes=LIMIT), **kw
    )


def inverse_norm(rows32):
    return 1.0 / jnp.sqrt(jnp.sum(rows32 * rows32, axis=1, keepdims=True) + 1e-06)


def unit(raw):
    rows32 = raw.astype(jnp.float32)
    return (rows32 * inverse_norm(rows32)).astype(jnp.bfloat16)


def pick_kernel(images, texts, out, sems):
    rows = out.shape[0]
    part = rows // sems.shape[0]

    def copy_from(src):
        copies = [
            pltpu.make_async_copy(
                src.at[pl.ds(i * part, part)], out.at[pl.ds(i * part, part)], sems.at[i]
            )
            for i in range(sems.shape[0])
        ]
        for copy in copies:
            copy.start()
        for copy in copies:
            copy.wait()

    @pl.when(is_even())
    def _():
        copy_from(texts)

    @pl.when(jnp.logical_not(is_even()))
    def _():
        copy_from(images)


def pick(images, texts):
    return call(
        pick_kernel,
        out_shape=jax.ShapeDtypeStruct(images.shape, images.dtype),
        in_specs=[HBM, HBM],
        out_specs=HBM,
        scratch_shapes=[pltpu.SemaphoreType.DMA((4,))],
        name="pick",
    )(images, texts)


def own_units_kernel(images, texts, u_raw, u_unit, v_unit):
    image_unit, text_unit = unit(images[...]), unit(texts[...])

    @pl.when(is_even())
    def _():
        u_raw[...] = images[...]
        u_unit[...] = image_unit
        v_unit[...] = text_unit

    @pl.when(jnp.logical_not(is_even()))
    def _():
        u_raw[...] = texts[...]
        u_unit[...] = text_unit
        v_unit[...] = image_unit


def own_units(images, texts):
    rows, width = images.shape
    tile = pl.BlockSpec((TILE, width), lambda i: (i, 0))
    shape = jax.ShapeDtypeStruct(images.shape, images.dtype)
    return call(
        own_units_kernel,
        grid=(rows // TILE,),
        out_shape=[shape] * 3,
        in_specs=[tile] * 2,
        out_specs=[tile] * 3,
        name="own_units",
    )(images, texts)


def units_kernel(raw, out):
    out[...] = unit(raw[...])


def units(raw):
    rows, width = raw.shape
    tile = pl.BlockSpec((TILE, width), lambda i: (i, 0))
    return call(
        units_kernel,
        grid=(rows // TILE,),
        out_shape=jax.ShapeDtypeStruct(raw.shape, raw.dtype),
        in_specs=[tile],
        out_specs=tile,
        name="units",
    )(raw)


def contribution(log_scale, bias, labels_x, labels_y, x, y):
    logits = lax.dot_general(x, y, (((1,), (1,)), ((), ())), preferred_element_type=jnp.float32)
    scale = jnp.exp(jnp.full((1, y.shape[0]), log_scale[0], jnp.float32))
    logits = scale * logits + bias[0]
    same = labels_x == labels_y
    size = scale / (1.0 + jnp.exp(jnp.where(same, logits, -logits)))
    coef = jnp.where(same, -size, size).astype(jnp.bfloat16)
    return jnp.dot(coef, y, preferred_element_type=jnp.float32)


def score_kernel(add, copy_x, pieces, *refs):
    log_scale, bias, labels_x, labels_y, x, y = refs[:6]
    refs = refs[6:]
    if add:
        before, refs = refs[0], refs[1:]
    out, refs = refs[0], refs[1:]
    if copy_x:
        x_again, refs = refs[0], refs[1:]
        x_again[...] = x[...]
    copies = []
    start = 0
    for i, size in enumerate(pieces):
        copies.append(
            pltpu.make_async_copy(
                y.at[pl.ds(start, size)], refs[i], refs[len(pieces)].at[i]
            )
        )
        start += size
    if pieces:

        @pl.when(pl.program_id(0) == 0)
        def _():
            for copy in copies:
                copy.start()

    grad = contribution(log_scale, bias, labels_x[...], labels_y[...], x[...], y[...])
    out[...] = before[...] + grad if add else grad
    if pieces:

        @pl.when(pl.program_id(0) == pl.num_programs(0) - 1)
        def _():
            for copy in copies:
                copy.wait()


def score(scalars, labels_x, labels_y, x, y, before=None, copy_x=False, pieces=()):
    rows, width = x.shape
    tile = pl.BlockSpec((TILE, width), lambda i: (i, 0))
    column = pl.BlockSpec((TILE, 1), lambda i: (i, 0))
    whole = pl.BlockSpec(y.shape, lambda i: (0, 0))
    line = pl.BlockSpec((1, y.shape[0]), lambda i: (0, 0))
    args = [*scalars, labels_x, labels_y, x, y]
    in_specs = [SMEM, SMEM, column, line, tile, whole]
    aliases = {}
    if before is not None:
        aliases = {len(args): 0}
        args.append(before)
        in_specs.append(tile)
    out_shape = [jax.ShapeDtypeStruct(x.shape, jnp.float32)]
    out_specs = [tile]
    if copy_x:
        out_shape.append(jax.ShapeDtypeStruct(x.shape, x.dtype))
        out_specs.append(tile)
    for size in pieces:
        out_shape.append(jax.ShapeDtypeStruct((size, width), y.dtype))
        out_specs.append(HBM)
    return call(
        functools.partial(score_kernel, before is not None, copy_x, pieces),
        grid=(rows // TILE,),
        out_shape=out_shape,
        in_specs=in_specs,
        out_specs=out_specs,
        input_output_aliases=aliases,
        scratch_shapes=[pltpu.SemaphoreType.DMA((len(pieces),))] if pieces else [],
        name="score",
    )(*args)


def finish_kernel(to_images_on_even, continued, *refs):
    log_scale, bias, labels_x, labels_y, x, y, before, raw = refs[:8]
    image_grad, text_grad, stage, sems = refs[10 if continued else 8 :]
    step = pl.program_id(0)
    grad = before[...] + contribution(
        log_scale, bias, labels_x[...], labels_y[...], x[...], y[...]
    )
    rows32 = raw[...].astype(jnp.float32)
    inverse = inverse_norm(rows32)
    exact = rows32 * inverse
    stage[step] = (grad - exact * jnp.sum(exact * grad, axis=1, keepdims=True)) * inverse
    to_images = is_even() if to_images_on_even else jnp.logical_not(is_even())

    def copy(out, i):
        return pltpu.make_async_copy(stage.at[i], out.at[pl.ds(i * TILE, TILE)], sems.at[i])

    for out, here in ((image_grad, to_images), (text_grad, jnp.logical_not(to_images))):

        @pl.when(here)
        def _(out=out):
            copy(out, step).start()

            @pl.when(step == pl.num_programs(0) - 1)
            def _():
                for i in range(stage.shape[0]):
                    copy(out, i).wait()


def finish(scalars, labels_x, labels_y, x, y, before, raw, to_images_on_even, outs=None):
    rows, width = x.shape
    tile = pl.BlockSpec((TILE, width), lambda i: (i, 0))
    column = pl.BlockSpec((TILE, 1), lambda i: (i, 0))
    whole = pl.BlockSpec(y.shape, lambda i: (0, 0))
    line = pl.BlockSpec((1, y.shape[0]), lambda i: (0, 0))
    args = [*scalars, labels_x, labels_y, x, y, before, raw]
    in_specs = [SMEM, SMEM, column, line, tile, whole, tile, tile]
    aliases = {}
    if outs is not None:
        aliases = {len(args): 0, len(args) + 1: 1}
        args += list(outs)
        in_specs += [HBM, HBM]
    return call(
        functools.partial(finish_kernel, to_images_on_even, outs is not None),
        grid=(rows // TILE,),
        out_shape=[jax.ShapeDtypeStruct(x.shape, jnp.float32)] * 2,
        in_specs=in_specs,
        out_specs=[HBM, HBM],
        input_output_aliases=aliases,
        scratch_shapes=[
            pltpu.VMEM((rows // TILE, TILE, width), jnp.float32),
            pltpu.SemaphoreType.DMA((rows // TILE,)),
        ],
        name="finish",
    )(*args)


def permute(value, even_step, odd_step):
    count = lax.axis_size(AXIS)
    pairs = [(p, (p + (odd_step if p % 2 else even_step)) % count) for p in range(count)]
    return lax.ppermute(value, AXIS, pairs)


def swap(value):
    return permute(value, 1, -1)


def on_device(images, texts, pair_ids, log_scale, bias):
    rows = images.shape[0]
    count = lax.axis_size(AXIS)
    me = lax.axis_index(AXIS)
    scalars = (log_scale, bias)

    v_raw = pick(images, texts)
    x_raw = permute(v_raw, -1, 1)

    all_ids = lax.all_gather(pair_ids, AXIS)
    sign = jnp.where(me % 2 == 0, 1, -1)
    away = sign * jnp.array([0, 1, -1, 2, 3, -2, -3], jnp.int32)
    near = all_ids[(me + away + count) % count]
    own, from_s0, from_x, from_s1, from_y, from_s2, from_z = [near[i : i + 1] for i in range(7)]
    labels = pair_ids.reshape(rows, 1)
    own = pair_ids.reshape(1, rows)

    u_raw, u_unit, v_unit = own_units(images, texts)
    s0 = swap(u_unit)
    (grad_u,) = score(scalars, labels, own, u_unit, v_unit)
    (grad_v,) = score(scalars, labels, own, v_unit, u_unit)
    grad_u, u_again = score(scalars, labels, from_s0, u_unit, s0, grad_u, copy_x=True)
    y = permute(u_again, 3, -3)

    x = units(x_raw)
    s1 = swap(x)
    grad_v, *parts = score(scalars, labels, from_x, v_unit, x, grad_v, pieces=PIECES)
    z = [permute(part, 2, -2) for part in parts]
    (grad_u,) = score(scalars, labels, from_s1, u_unit, s1, grad_u)

    s2 = swap(y)
    outs = finish(scalars, labels, from_y, u_unit, y, grad_u, u_raw, True)
    (grad_v,) = score(scalars, labels, from_s2, v_unit, s2, grad_v)

    start = 0
    for size, part in zip(PIECES, z):
        here = from_z[:, start : start + size]
        start += size
        if start < rows:
            (grad_v,) = score(scalars, labels, here, v_unit, part, grad_v)
        else:
            outs = finish(scalars, labels, here, v_unit, part, grad_v, v_raw, False, outs)
    return tuple(outs)


def solution(mesh):
    in_specs = (P("dp", None), P("dp", None), P("dp"), P(), P())
    out_specs = (P("dp", None), P("dp", None))
    return jax.shard_map(
        on_device, mesh=mesh, in_specs=in_specs, out_specs=out_specs, check_vma=False
    )
```

time: 344 us -> 157 us (0.46)
  the two profiles are of different devices: /device:TPU:0 before, /device:TPU:1 now
where the time goes in v1:
time: 157 us
  Pallas kernels  62.6 us (40%)
  blocking collectives  54.7 us (35%)
  waiting for transfers between devices  20.3 us (13%)
  starting transfers between devices  12.1 us (8%)
  local copies, waits for them, and re-layouts  4.95 us (3%)
  between operations  2.33 us (1%)
    all_gather x1, blocking collectives, on_device(): all_ids = lax.all_gather(pair_ids, AXIS)  54.7 us
    pallas_call x8, Pallas kernels, score(): call(functools.partial(score_kernel, before is not None, copy_x, pieces),...  42.2 us
    ppermute x8, waiting for transfers between devices, permute(): return lax.ppermute(value, AXIS, pairs)  20.3 us
    pallas_call x2, Pallas kernels, finish(): call(functools.partial(finish_kernel, to_images_on_even, outs is not None...  13.6 us
    ppermute x8, starting transfers between devices, permute(): return lax.ppermute(value, AXIS, pairs)  12.1 us
    unnamed x14, local copies, waits for them, and re-layouts  4.2 us
  transfers between devices with their start and end apart: 8, of which 1 were waited for; matrix products, arithmetic and copies ran while one was open for 1% of the time, Pallas kernels for 34%

profile of v1, /device:TPU:1, one launch (start us, length us, event | category | flops | bytes accessed | tf_op | source)
XLA Modules:
  0.0 157.0 jit_solution(16269885948734593466)
XLA Ops:
  0.6 0.0 copy-start
  0.6 1.5 copy-done
  2.1 0.0 copy-start.1
  2.1 1.5 copy-done.1
  3.6 2.9 %own_units.1 = (bf16[768,1152]{1,0:T(8,128)(2,1)S(1)}, bf16[768,1152]{1,0:T(8,128)(2,1)}, bf16[768,1152]{1,0:T(8,128)(2,1)S(1)}) custom-call(bf16[768,1152]{1,0:T(8,128)(2,1)S(1)} %copy-done, bf16[768,1152]{1,0:T(8,128)(2,1)S(1)} %copy-done.1), custom_call_target="tpu_custom_call" | custom-call | tf_op jit(solution)/shard_map/own_units/pallas_call | solution.py:93
  6.5 0.0 copy-start.2
  6.5 1.2 copy-done.2
  7.7 0.0 copy-start.4
  7.7 0.0 copy-start.5
  7.7 1.4 collective-permute-start.4
  9.1 1.3 pick.1.refs_7_
  10.4 1.3 collective-permute-start
  11.7 0.0 copy-done.4
  11.7 0.2 reshape.22.refs_2_
  12.5 54.7 %all-gather.1 = s32[128,1,768]{2,1,0:T(1,128)S(1)} all-gather(s32[1,1,768]{2,1,0:T(1,128)S(1)} %reshape.19), channel_id=2, replica_groups=mesh['dp'=128] {'dp'}, dimensions={0}, use_global_device_ids=true | all-gather | bytes 396288 | tf_op jit(solution)/shard_map/all_gather | solution.py:273
  67.3 0.0 copy-done.5
  67.3 0.6 gather_fusion
  68.5 5.9 %score.10.refs_6_ = f32[768,1152]{1,0:T(8,128)S(1)} custom-call(f32[1]{0:T(128)S(6)} %copy.47.refs_0_, f32[1]{0:T(128)S(6)} %copy.48.refs_1_, s32[768,1]{1,0:T(8,128)S(1)} %reshape.22.refs_2_, s32[1,768]{1,0:T(1,128)S(1)} %all_gather.6.refs_3_, bf16[768,1152]{1,0:T(8,128)(2,1)} %get-tuple-element.14.refs_5_.refs_4_, ...), custom_call_target="tpu_custom_call" | custom-call | tf_op jit(solution)/shard_map/score/pallas_call | solution.py:186
  74.4 0.0 collective-permute-done.4.refs_5_
  74.4 6.8 %score.11 = (f32[768,1152]{1,0:T(8,128)S(1)}, bf16[768,1152]{1,0:T(8,128)(2,1)S(1)}) custom-call(f32[1]{0:T(128)S(6)} %copy.47.refs_0_, f32[1]{0:T(128)S(6)} %copy.48.refs_1_, s32[768,1]{1,0:T(8,128)S(1)} %reshape.22.refs_2_, s32[1,768]{1,0:T(1,128)S(1)} %get-tuple-element.26.refs_3_, ...), custom_call_target="tpu_custom_call", output_to_operand_aliasing={{0}: (6, {})} | custom-call | tf_op jit(solution)/shard_map/score/pallas_call | solution.py:186
  81.3 4.4 %collective-permute-start.5 = (bf16[768,1152]{1,0:T(8,128)(2,1)S(1)}, bf16[768,1152]{1,0:T(8,128)(2,1)S(1)}, u32[]{:S(2)}, u32[]{:S(2)}) collective-permute-start(bf16[768,1152]{1,0:T(8,128)(2,1)S(1)} %get-tuple-element.18), channel_id=1, source_target_pairs={{0,3},{1,126},{2,5},{3,0},{4,7},{5,2},{6,9},{7,4},{8,11},{9,6},{10... | collective-permute-start | bytes 5308424 | tf_op jit(solution)/shard_map/ppermute | solution.py:257
  85.7 0.0 collective-permute-done.raw
  85.7 2.6 %units.1.refs_5_ = bf16[768,1152]{1,0:T(8,128)(2,1)S(1)} custom-call(bf16[768,1152]{1,0:T(8,128)(2,1)} %collective-permute-done.raw), custom_call_target="tpu_custom_call" | custom-call | tf_op jit(solution)/shard_map/units/pallas_call | solution.py:110
  88.3 0.1 collective-permute-start.7
  88.4 20.3 %collective-permute-done.5.refs_5_ = bf16[768,1152]{1,0:T(8,128)(2,1)S(1)} collective-permute-done((bf16[768,1152]{1,0:T(8,128)(2,1)S(1)}, bf16[768,1152]{1,0:T(8,128)(2,1)S(1)}, u32[]{:S(2)}, u32[]{:S(2)}) %collective-permute-start.5) | collective-permute-done | bytes 1769504 | tf_op jit(solution)/shard_map/ppermute | solution.py:257
  108.7 0.0 collective-permute-start.6
  108.7 6.2 %score.8.refs_6_ = f32[768,1152]{1,0:T(8,128)S(1)} custom-call(f32[1]{0:T(128)S(6)} %copy.47.refs_0_, f32[1]{0:T(128)S(6)} %copy.48.refs_1_, s32[768,1]{1,0:T(8,128)S(1)} %reshape.22.refs_2_, s32[1,768]{1,0:T(1,128)S(1)} %all_gather.6.refs_3_, bf16[768,1152]{1,0:T(8,128)(2,1)S(1)} %get-tuple-element.13.refs_4_.refs_5_, ...), custom_call_target="tpu_custom_call" | custom-call | tf_op jit(solution)/shard_map/score/pallas_call | solution.py:186
  115.0 5.6 %score.9 = (f32[768,1152]{1,0:T(8,128)S(1)}, bf16[384,1152]{1,0:T(8,128)(2,1)S(1)}, bf16[256,1152]{1,0:T(8,128)(2,1)S(1)}, bf16[128,1152]{1,0:T(8,128)(2,1)S(1)}) custom-call(f32[1]{0:T(128)S(6)} %copy.47.refs_0_, f32[1]{0:T(128)S(6)} %copy.48.refs_1_, s32[768,1]{1,0:T(8,128)S(1)} %reshape.22.refs_2_, ...), custom_call_target="tpu_custom_call", output_to_operand_aliasing={{0}: (6, {})} | custom-call | tf_op jit(solution)/shard_map/score/pallas_call | solution.py:186
  120.6 4.5 %collective-permute-start.3 = (bf16[384,1152]{1,0:T(8,128)(2,1)S(1)}, bf16[384,1152]{1,0:T(8,128)(2,1)S(1)}, u32[]{:S(2)}, u32[]{:S(2)}) collective-permute-start(bf16[384,1152]{1,0:T(8,128)(2,1)S(1)} %get-tuple-element.17), channel_id=1, source_target_pairs={{0,2},{1,127},{2,4},{3,1},{4,6},{5,3},{6,8},{7,5},{8,10},{9,7},{10... | collective-permute-start | bytes 2654216 | tf_op jit(solution)/shard_map/ppermute | solution.py:257
  125.1 0.1 collective-permute-start.2
  125.2 0.3 collective-permute-start.1
  125.5 0.0 collective-permute-done.7.refs_5_
  125.5 0.0 copy-start.3
  125.5 6.3 %score.15.refs_6_ = f32[768,1152]{1,0:T(8,128)S(1)} custom-call(f32[1]{0:T(128)S(6)} %copy.47.refs_0_, f32[1]{0:T(128)S(6)} %copy.48.refs_1_, s32[768,1]{1,0:T(8,128)S(1)} %reshape.22.refs_2_, s32[1,768]{1,0:T(1,128)S(1)} %get-tuple-element.24.refs_3_, bf16[768,1152]{1,0:T(8,128)(2,1)} %get-tuple-element.14.refs_5_.refs_4_, ...), custom_call_target="tpu_custom_call", output_to_operand_aliasing={{}: (6, {})} | custom-call | tf_op jit(solution)/shard_map/score/pallas_call | solution.py:186
  131.8 0.0 copy-done.3
  131.8 7.9 %finish.2 = (f32[768,1152]{1,0:T(8,128)}, f32[768,1152]{1,0:T(8,128)}) custom-call(f32[1]{0:T(128)S(6)} %copy.47.refs_0_, f32[1]{0:T(128)S(6)} %copy.48.refs_1_, s32[768,1]{1,0:T(8,128)S(1)} %reshape.22.refs_2_, s32[1,768]{1,0:T(1,128)S(1)} %get-tuple-element.25.refs_3_, bf16[768,1152]{1,0:T(8,128)(2,1)} %get-tuple-element.14.refs_5_.refs_4_, ...), custom_call_target="tpu_custom_call" | custom-call | tf_op jit(solution)/shard_map/finish/pallas_call | solution.py:239
  139.7 0.0 collective-permute-done.6.refs_5_
  139.7 5.2 %score.12.refs_6_ = f32[768,1152]{1,0:T(8,128)S(1)} custom-call(f32[1]{0:T(128)S(6)} %copy.47.refs_0_, f32[1]{0:T(128)S(6)} %copy.48.refs_1_, s32[768,1]{1,0:T(8,128)S(1)} %reshape.22.refs_2_, s32[1,768]{1,0:T(1,128)S(1)} %get-tuple-element.27.refs_3_, bf16[768,1152]{1,0:T(8,128)(2,1)S(1)} %get-tuple-element.13.refs_4_.refs_5_, ...), custom_call_target="tpu_custom_call", output_to_operand_aliasing={{}: (6, {})} | custom-call | tf_op jit(solution)/shard_map/score/pallas_call | solution.py:186
  144.9 0.0 collective-permute-done.3.refs_5_
  144.9 3.2 %score.13.refs_6_ = f32[768,1152]{1,0:T(8,128)S(1)} custom-call(f32[1]{0:T(128)S(6)} %copy.47.refs_0_, f32[1]{0:T(128)S(6)} %copy.48.refs_1_, s32[768,1]{1,0:T(8,128)S(1)} %reshape.22.refs_2_, s32[1,384]{1,0:T(1,128)S(1)} %slice.41.refs_3_, bf16[768,1152]{1,0:T(8,128)(2,1)S(1)} %get-tuple-element.13.refs_4_.refs_5_, ...), custom_call_target="tpu_custom_call", output_to_operand_aliasing={{}: (6, {})} | custom-call | tf_op jit(solution)/shard_map/score/pallas_call | solution.py:186
  148.1 0.0 collective-permute-done.2.refs_5_
  148.1 3.0 %score.14.refs_6_ = f32[768,1152]{1,0:T(8,128)S(1)} custom-call(f32[1]{0:T(128)S(6)} %copy.47.refs_0_, f32[1]{0:T(128)S(6)} %copy.48.refs_1_, s32[768,1]{1,0:T(8,128)S(1)} %reshape.22.refs_2_, s32[1,256]{1,0:T(1,128)S(1)} %slice.40.refs_3_, bf16[768,1152]{1,0:T(8,128)(2,1)S(1)} %get-tuple-element.13.refs_4_.refs_5_, ...), custom_call_target="tpu_custom_call", output_to_operand_aliasing={{}: (6, {})} | custom-call | tf_op jit(solution)/shard_map/score/pallas_call | solution.py:186
  151.1 0.0 collective-permute-done.1.refs_5_
  151.2 5.7 %finish.3 = (f32[768,1152]{1,0:T(8,128)}, f32[768,1152]{1,0:T(8,128)}) custom-call(f32[1]{0:T(128)S(6)} %copy.47.refs_0_, f32[1]{0:T(128)S(6)} %copy.48.refs_1_, s32[768,1]{1,0:T(8,128)S(1)} %reshape.22.refs_2_, s32[1,128]{1,0:T(1,128)S(1)} %slice.38.refs_3_, ...), custom_call_target="tpu_custom_call", output_to_operand_aliasing={{0}: (8, {}), {1}: (9, {})} | custom-call | tf_op jit(solution)/shard_map/finish/pallas_call | solution.py:239
  (9 shorter events, 0.1 us)
Async XLA Ops:
  0.6 1.5 copy-start
  2.1 1.5 copy-start.1
  6.5 1.2 copy-start.2
  7.7 4.0 %copy-start.4 = (s32[768]{0:T(1024)S(1)}, s32[768]{0:T(1024)}, u32[]{:S(2)}) copy-start(s32[768]{0:T(1024)} %param.8) | copy-start | bytes 9220
  7.7 59.6 %copy-start.5 = (s32[7]{0:T(128)S(1)}, s32[7]{0:T(128)}, u32[]{:S(2)}) copy-start(s32[7]{0:T(128)} %constant.39.clone) | copy-start | bytes 88
  7.7 66.7 %collective-permute-start.4 = (bf16[768,1152]{1,0:T(8,128)(2,1)}, bf16[768,1152]{1,0:T(8,128)(2,1)}, u32[]{:S(2)}, u32[]{:S(2)}) collective-permute-start(bf16[768,1152]{1,0:T(8,128)(2,1)} %get-tuple-element.14.refs_5_.refs_4_), channel_id=1, source_target_pairs={{0,1},{1,0},{2,3},{3,2},{4,5},{5,4},{6,7},{7,6},{8,9},{9,8},{10,11... | collective-permute-start | bytes 5308424 | tf_op jit(solution)/shard_map/ppermute | solution.py:257
  10.4 75.3 %collective-permute-start = (bf16[768,1152]{1,0:T(8,128)(2,1)}, bf16[768,1152]{1,0:T(8,128)(2,1)}, u32[]{:S(2)}, u32[]{:S(2)}) collective-permute-start(bf16[768,1152]{1,0:T(8,128)(2,1)} %pick.1.refs_7_), channel_id=1, source_target_pairs={{0,127},{1,2},{2,1},{3,4},{4,3},{5,6},{6,5},{7,8},{8,7},{9,10},{10... | collective-permute-start | bytes 5308424 | tf_op jit(solution)/shard_map/ppermute | solution.py:257
  81.3 27.5 %collective-permute-start.5 = (bf16[768,1152]{1,0:T(8,128)(2,1)S(1)}, bf16[768,1152]{1,0:T(8,128)(2,1)S(1)}, u32[]{:S(2)}, u32[]{:S(2)}) collective-permute-start(bf16[768,1152]{1,0:T(8,128)(2,1)S(1)} %get-tuple-element.18), channel_id=1, source_target_pairs={{0,3},{1,126},{2,5},{3,0},{4,7},{5,2},{6,9},{7,4},{8,11},{9,6},{10... | collective-permute-start | bytes 5308424 | tf_op jit(solution)/shard_map/ppermute | solution.py:257
  88.3 37.1 %collective-permute-start.7 = (bf16[768,1152]{1,0:T(8,128)(2,1)S(1)}, bf16[768,1152]{1,0:T(8,128)(2,1)S(1)}, u32[]{:S(2)}, u32[]{:S(2)}) collective-permute-start(bf16[768,1152]{1,0:T(8,128)(2,1)S(1)} %units.1.refs_5_), channel_id=1, source_target_pairs={{0,1},{1,0},{2,3},{3,2},{4,5},{5,4},{6,7},{7,6},{8,9},{9,8},{10,11... | collective-permute-start | bytes 5308424 | tf_op jit(solution)/shard_map/ppermute | solution.py:257
  108.7 31.0 %collective-permute-start.6 = (bf16[768,1152]{1,0:T(8,128)(2,1)S(1)}, bf16[768,1152]{1,0:T(8,128)(2,1)S(1)}, u32[]{:S(2)}, u32[]{:S(2)}) collective-permute-start(bf16[768,1152]{1,0:T(8,128)(2,1)S(1)} %collective-permute-done.5.refs_5_), channel_id=1, source_target_pairs={{0,1},{1,0},{2,3},{3,2},{4,5},{5,4},{6,7},{7,6},{8,9},{9,8},{10,11... | collective-permute-start | bytes 5308424 | tf_op jit(solution)/shard_map/ppermute | solution.py:257
  120.6 24.4 %collective-permute-start.3 = (bf16[384,1152]{1,0:T(8,128)(2,1)S(1)}, bf16[384,1152]{1,0:T(8,128)(2,1)S(1)}, u32[]{:S(2)}, u32[]{:S(2)}) collective-permute-start(bf16[384,1152]{1,0:T(8,128)(2,1)S(1)} %get-tuple-element.17), channel_id=1, source_target_pairs={{0,2},{1,127},{2,4},{3,1},{4,6},{5,3},{6,8},{7,5},{8,10},{9,7},{10... | collective-permute-start | bytes 2654216 | tf_op jit(solution)/shard_map/ppermute | solution.py:257
  125.1 23.0 %collective-permute-start.2 = (bf16[256,1152]{1,0:T(8,128)(2,1)S(1)}, bf16[256,1152]{1,0:T(8,128)(2,1)S(1)}, u32[]{:S(2)}, u32[]{:S(2)}) collective-permute-start(bf16[256,1152]{1,0:T(8,128)(2,1)S(1)} %get-tuple-element.16), channel_id=1, source_target_pairs={{0,2},{1,127},{2,4},{3,1},{4,6},{5,3},{6,8},{7,5},{8,10},{9,7},{10... | collective-permute-start | bytes 1769480 | tf_op jit(solution)/shard_map/ppermute | solution.py:257
  125.2 25.9 %collective-permute-start.1 = (bf16[128,1152]{1,0:T(8,128)(2,1)S(1)}, bf16[128,1152]{1,0:T(8,128)(2,1)S(1)}, u32[]{:S(2)}, u32[]{:S(2)}) collective-permute-start(bf16[128,1152]{1,0:T(8,128)(2,1)S(1)} %get-tuple-element.15), channel_id=1, source_target_pairs={{0,2},{1,127},{2,4},{3,1},{4,6},{5,3},{6,8},{7,5},{8,10},{9,7},{10... | collective-permute-start | bytes 884744 | tf_op jit(solution)/shard_map/ppermute | solution.py:257
  125.5 6.3 %copy-start.3 = (bf16[768,1152]{1,0:T(8,128)(2,1)S(1)}, bf16[768,1152]{1,0:T(8,128)(2,1)}, u32[]{:S(2)}) copy-start(bf16[768,1152]{1,0:T(8,128)(2,1)} %copy-done.2) | copy-start | bytes 5308420

commit v2 on v0

v2 whole, which is shorter than its diff:
```python
import functools

import jax
import jax.numpy as jnp
from jax import lax
from jax.experimental import pallas as pl
from jax.experimental.pallas import tpu as pltpu
from jax.sharding import PartitionSpec as P

AXIS = "dp"
TILE = 256
ROWS = 768
LABEL_ROWS = 16
PIECES = (384, 256, 128)
PARTS = 4
LIMIT = 16 * 1024 * 1024
LOG2E = 1.4426950408889634
MICROSECOND = 1.0e9
ANY = pl.BlockSpec(memory_space=pl.ANY)
HBM = pl.BlockSpec(memory_space=pltpu.HBM)
VMEM = pl.BlockSpec(memory_space=pltpu.VMEM)
SMEM = pl.BlockSpec(memory_space=pltpu.SMEM)


def is_even():
    return lax.rem(lax.axis_index(AXIS), 2) == 0


def call(kernel, args, in_specs, out_shape, cost=1, **kw):
    places = {id(VMEM): pltpu.VMEM, id(HBM): pltpu.HBM}
    args = [
        pltpu.with_memory_space_constraint(arg, places[id(spec)]) if id(spec) in places else arg
        for arg, spec in zip(args, in_specs)
    ]
    return pl.pallas_call(
        kernel,
        out_shape=out_shape,
        in_specs=in_specs,
        compiler_params=pltpu.CompilerParams(vmem_limit_bytes=LIMIT),
        cost_estimate=pl.CostEstimate(
            flops=int(cost * MICROSECOND), bytes_accessed=0, transcendentals=0
        ),
        **kw,
    )(*args)


def inverse_norm(rows32):
    return 1.0 / jnp.sqrt(jnp.sum(rows32 * rows32, axis=1, keepdims=True) + 1e-06)


def unit(raw):
    rows32 = raw.astype(jnp.float32)
    return (rows32 * inverse_norm(rows32)).astype(jnp.bfloat16)


def put_units(raw, out):
    for start in range(0, ROWS, TILE):
        rows = pl.ds(start, TILE)
        out[rows, :] = unit(raw[rows, :])
    out[ROWS:, :] = raw[ROWS:, :]


def put_labels(ids, out):
    out[ROWS:, :] = jnp.zeros((LABEL_ROWS, out.shape[1]), out.dtype)
    labels = jnp.broadcast_to(ids[...], (LABEL_ROWS, ROWS)).astype(jnp.float32)
    out[ROWS:, :ROWS] = labels.astype(out.dtype)


def pick_copies(src, out, sems):
    part = ROWS // PARTS
    return [
        pltpu.make_async_copy(
            src.at[pl.ds(i * part, part)], out.at[pl.ds(i * part, part)], sems.at[i]
        )
        for i in range(PARTS)
    ]


def start_pick(take_texts, images, texts, out, sems):
    for src, here in ((texts, take_texts), (images, jnp.logical_not(take_texts))):

        @pl.when(here)
        def _(src=src):
            for copy in pick_copies(src, out, sems):
                copy.start()


def wait_pick(images, out, sems):
    for copy in pick_copies(images, out, sems):
        copy.wait()


def first_kernel(images, texts, ids, v_raw, sems):
    start_pick(is_even(), images, texts, v_raw, sems)
    put_labels(ids, v_raw)
    wait_pick(images, v_raw, sems)


def first(images, texts, ids):
    return call(
        first_kernel,
        [images, texts, ids],
        [HBM, HBM, VMEM],
        pltpu.VMEM((ROWS + LABEL_ROWS, images.shape[1]), images.dtype),
        out_specs=VMEM,
        scratch_shapes=[pltpu.SemaphoreType.DMA((PARTS,))],
        name="first",
    )


def second_kernel(images, texts, ids, v_raw, u_raw, u, v, sems):
    start_pick(jnp.logical_not(is_even()), images, texts, u_raw, sems)
    put_labels(ids, u_raw)
    put_units(v_raw, v)
    wait_pick(images, u_raw, sems)
    put_units(u_raw, u)


def second(images, texts, ids, v_raw):
    return call(
        second_kernel,
        [images, texts, ids, v_raw],
        [HBM, HBM, VMEM, VMEM],
        [pltpu.VMEM(v_raw.shape, v_raw.dtype)] * 3,
        out_specs=[VMEM] * 3,
        scratch_shapes=[pltpu.SemaphoreType.DMA((PARTS,))],
        name="second",
        cost=2,
    )


def units(raw):
    return call(
        put_units,
        [raw],
        [VMEM],
        pltpu.VMEM(raw.shape, raw.dtype),
        out_specs=VMEM,
        name="units",
        cost=0.7,
    )


def cut_kernel(value, later, *outs):
    start = 0
    for out in outs:
        size = out.shape[0] if len(outs) == 1 or start else out.shape[0] - LABEL_ROWS
        out[:size, :] = value[pl.ds(start, size), :]
        if size < out.shape[0]:
            out[size:, :] = value[ROWS:, :]
        start += size


def cut(value, later, sizes):
    return call(
        cut_kernel,
        [value, later],
        [VMEM, ANY],
        [pltpu.VMEM((size, value.shape[1]), value.dtype) for size in sizes],
        out_specs=[VMEM] * len(sizes),
        name="cut",
        cost=0.2,
    )


def contributions(log_scale, bias, labels_x, labels_y, x, y, size):
    scale = jnp.exp(jnp.full((1, size), log_scale[0], jnp.float32))
    rate = scale * -LOG2E
    shift = bias[0] * -LOG2E
    tiles = [pl.ds(start, TILE) for start in range(0, ROWS, TILE)]

    def products(rows):
        return lax.dot_general(
            x[rows, :], y[:size, :], (((1,), (1,)), ((), ())), preferred_element_type=jnp.float32
        )

    ahead = products(tiles[0])
    for i, rows in enumerate(tiles):
        now = ahead
        if i + 1 < len(tiles):
            ahead = products(tiles[i + 1])
        sigmoid = 1.0 / (1.0 + jnp.exp2(now * rate + shift))
        same = jnp.where(labels_x[rows, :] == labels_y, 1.0, 0.0)
        coef = ((sigmoid - same) * scale).astype(jnp.bfloat16)
        yield rows, jnp.dot(coef, y[:size, :], preferred_element_type=jnp.float32)


def line_of(labelled, labels_at, start, size):
    lines = labelled[labels_at : labels_at + LABEL_ROWS, :].astype(jnp.float32)
    return lines[:1, start : start + size]


def score_kernel(where, log_scale, bias, labels_x, x, y, *refs):
    labels_at, start, size = where
    labelled = y
    if labels_at + LABEL_ROWS > y.shape[0]:
        labelled, refs = refs[0], refs[1:]
    out = refs[-1]
    labels_y = line_of(labelled, labels_at, start, size)
    for rows, grad in contributions(log_scale, bias, labels_x, labels_y, x, y, size):
        out[rows, :] = refs[0][rows, :] + grad if len(refs) > 1 else grad


def score_args(scalars, labels_x, x, y, labelled, labels_at, start):
    size = y.shape[0] if labelled is not None else labels_at
    args = [*scalars, labels_x, x, y] + ([labelled] if labelled is not None else [])
    in_specs = [SMEM, SMEM] + [VMEM] * (len(args) - 2)
    cost = 3.5 * size / ROWS
    return args, in_specs, (labels_at, start, size), cost


def score(scalars, labels_x, x, y, before=None, labelled=None, labels_at=ROWS, start=0):
    args, in_specs, where, cost = score_args(
        scalars, labels_x, x, y, labelled, labels_at, start
    )
    aliases = {}
    if before is not None:
        aliases = {len(args): 0}
        args.append(before)
        in_specs.append(VMEM)
    return call(
        functools.partial(score_kernel, where),
        args,
        in_specs,
        pltpu.VMEM((ROWS, x.shape[1]), jnp.float32),
        out_specs=VMEM,
        input_output_aliases=aliases,
        name="score",
        cost=cost,
    )


def finish_kernel(where, to_images_on_even, continued, *refs):
    labels_at, start, size = where
    log_scale, bias, labels_x, x, y = refs[:5]
    refs = refs[5:]
    labelled = y
    if labels_at + LABEL_ROWS > y.shape[0]:
        labelled, refs = refs[0], refs[1:]
    before, raw = refs[:2]
    image_grad, text_grad, stage, sems = refs[4 if continued else 2 :]
    to_images = is_even() if to_images_on_even else jnp.logical_not(is_even())
    places = ((image_grad, to_images), (text_grad, jnp.logical_not(to_images)))

    def copy(out, rows, i):
        return pltpu.make_async_copy(stage.at[rows], out.at[rows], sems.at[i])

    labels_y = line_of(labelled, labels_at, start, size)
    steps = []
    for rows, grad in contributions(log_scale, bias, labels_x, labels_y, x, y, size):
        grad = before[rows, :] + grad
        rows32 = raw[rows, :].astype(jnp.float32)
        inverse = inverse_norm(rows32)
        exact = rows32 * inverse
        stage[rows, :] = (grad - exact * jnp.sum(exact * grad, axis=1, keepdims=True)) * inverse
        for out, here in places:
            pl.when(here)(copy(out, rows, len(steps)).start)
        steps.append(rows)
    for i, rows in enumerate(steps):
        copy(image_grad, rows, i).wait()


def finish(
    scalars,
    labels_x,
    x,
    y,
    before,
    raw,
    to_images_on_even,
    outs=None,
    labelled=None,
    labels_at=ROWS,
    start=0,
):
    args, in_specs, where, cost = score_args(
        scalars, labels_x, x, y, labelled, labels_at, start
    )
    args += [before, raw]
    in_specs += [VMEM, VMEM]
    aliases = {}
    if outs is not None:
        aliases = {len(args): 0, len(args) + 1: 1}
        args += list(outs)
        in_specs += [HBM, HBM]
    shape = (ROWS, x.shape[1])
    return call(
        functools.partial(finish_kernel, where, to_images_on_even, outs is not None),
        args,
        in_specs,
        [pltpu.HBM(shape, jnp.float32)] * 2,
        out_specs=[HBM, HBM],
        input_output_aliases=aliases,
        scratch_shapes=[
            pltpu.VMEM(shape, jnp.float32),
            pltpu.SemaphoreType.DMA((ROWS // TILE,)),
        ],
        name="finish",
        cost=cost + 2,
    )


def permute(value, even_step, odd_step):
    count = lax.axis_size(AXIS)
    pairs = [(p, (p + (odd_step if p % 2 else even_step)) % count) for p in range(count)]
    return lax.ppermute(value, AXIS, pairs)


def swap(value):
    return permute(value, 1, -1)


def on_device(images, texts, pair_ids, log_scale, bias):
    scalars = (log_scale, bias)
    ids = pair_ids.reshape(1, ROWS)
    labels = pair_ids.astype(jnp.float32).reshape(ROWS, 1)

    v_raw = first(images, texts, ids)
    x_raw = permute(v_raw, -1, 1)
    u_raw, u, v = second(images, texts, ids, v_raw)
    s0 = swap(u)
    grad_u = score(scalars, labels, u, v)
    grad_v = score(scalars, labels, v, u)
    (u_again,) = cut(u, grad_v, (u.shape[0],))
    y = permute(u_again, 3, -3)
    grad_u = score(scalars, labels, u, s0, grad_u)

    x = units(x_raw)
    s1 = swap(x)
    grad_v = score(scalars, labels, v, x, grad_v)
    grad_u = score(scalars, labels, u, s1, grad_u)
    sizes = (PIECES[0] + LABEL_ROWS, *PIECES[1:])
    z = [permute(piece, 2, -2) for piece in cut(x, grad_u, sizes)]

    s2 = swap(y)
    outs = finish(scalars, labels, u, y, grad_u, u_raw, True)
    grad_v = score(scalars, labels, v, s2, grad_v)

    grad_v = score(scalars, labels, v, z[0], grad_v, labels_at=PIECES[0])
    start = PIECES[0]
    for piece in z[1:]:
        place = dict(labelled=z[0], labels_at=PIECES[0], start=start)
        start += piece.shape[0]
        if start < ROWS:
            grad_v = score(scalars, labels, v, piece, grad_v, **place)
        else:
            outs = finish(scalars, labels, v, piece, grad_v, v_raw, False, outs, **place)
    return tuple(outs)


def solution(mesh):
    in_specs = (P("dp", None), P("dp", None), P("dp"), P(), P())
    out_specs = (P("dp", None), P("dp", None))
    return jax.shard_map(
        on_device, mesh=mesh, in_specs=in_specs, out_specs=out_specs, check_vma=False
    )
```

time: 344 us -> 94.8 us (0.28)
  waiting for transfers between devices: 284 us -> 35.3 us
  Pallas kernels: 0 us -> 39.9 us
  matrix products: 23.3 us -> 0 us
  other arithmetic: 9.87 us -> 0.01 us
  starting transfers between devices: 24.8 us -> 16.1 us
    ppermute x10 -> x8, waiting for transfers between devices: 284 us -> 35.3 us  [permute(): return lax.ppermute(value, AXIS, pairs)]
    pallas_call x0 -> x15, Pallas kernels: none -> 39.9 us  [call(): pl.pallas_call(kernel, out_shape=out_shape, in_specs=in_specs, compiler_p...]
    dot_general x12 -> x0, matrix products: 23.3 us -> none  [the longest x4 8.95 us: weights(): lax.dot_general(image_block, text_block, (((1,), (1,)), ((), ())), prefer...]
    ppermute x10 -> x8, starting transfers between devices: 24.8 us -> 16.1 us  [permute(): return lax.ppermute(value, AXIS, pairs)]
    div x2 -> x0, other arithmetic: 4.94 us -> none  [back_through(): return (grad - exact * jnp.sum(exact * grad, axis=1, keepdims=True)) / norms]
  transfers between devices with their start and end apart: 10 -> 8, of which waited for: 4 -> 5; matrix products, arithmetic and copies ran while one was open for 6% -> 0% of each run, Pallas kernels for 0% -> 37%
where the time goes in v2:
time: 94.8 us; the launch traced here: 94.5 us
  Pallas kernels  39.9 us (42%)
  waiting for transfers between devices  35.3 us (37%)
  starting transfers between devices  16.1 us (17%)
  between operations  2.28 us (2%)
    pallas_call x15, Pallas kernels, call(): pl.pallas_call(kernel, out_shape=out_shape, in_specs=in_specs, compiler_p...  39.9 us
    ppermute x8, waiting for transfers between devices, permute(): return lax.ppermute(value, AXIS, pairs)  35.3 us
    ppermute x8, starting transfers between devices, permute(): return lax.ppermute(value, AXIS, pairs)  16.1 us
  transfers between devices with their start and end apart: 8, of which 5 were waited for; matrix products, arithmetic and copies ran while one was open for 0% of the time, Pallas kernels for 37%

profile of v2, /device:TPU:0, one launch (start us, length us, event | category | flops | bytes accessed | tf_op | source)
XLA Modules:
  0.0 94.5 jit_solution(13831630730800902144)
XLA Ops:
  0.6 0.7 reshape.11.ids
  1.3 0.0 copy-start
  1.3 1.5 %first.1.v_raw.refs_7_ = bf16[784,1152]{1,0:T(8,128)(2,1)S(1)} custom-call(bf16[768,1152]{1,0:T(8,128)(2,1)} %images.3, bf16[768,1152]{1,0:T(8,128)(2,1)} %texts.3, s32[1,768]{1,0:T(1,128)S(1)} %reshape.11.ids), custom_call_target="tpu_custom_call" | custom-call | flops 1000000000 | tf_op jit(solution)/shard_map/first/pallas_call | solution.py:35
  2.8 8.3 %collective-permute-start = (bf16[784,1152]{1,0:T(8,128)(2,1)S(1)}, bf16[784,1152]{1,0:T(8,128)(2,1)S(1)}, u32[]{:S(2)}, u32[]{:S(2)}) collective-permute-start(bf16[784,1152]{1,0:T(8,128)(2,1)S(1)} %first.1.v_raw.refs_7_), channel_id=1, source_target_pairs={{0,127},{1,2},{2,1},{3,4},{4,3},{5,6},{6,5},{7,8},{8,7},{9,10},{10... | collective-permute-start | bytes 5419016 | tf_op jit(solution)/shard_map/ppermute | solution.py:306
  11.1 0.0 copy-done
  11.1 0.2 reshape.12.labels_x.refs_2_
  12.6 2.1 %second.1 = (bf16[784,1152]{1,0:T(8,128)(2,1)S(1)}, bf16[784,1152]{1,0:T(8,128)(2,1)S(1)}, bf16[784,1152]{1,0:T(8,128)(2,1)S(1)}) custom-call(bf16[768,1152]{1,0:T(8,128)(2,1)} %images.3, bf16[768,1152]{1,0:T(8,128)(2,1)} %texts.3, s32[1,768]{1,0:T(1,128)S(1)} %reshape.11.ids, bf16[784,1152]{1,0:T(8,128)(2,1)S(1)} %first.1.v_raw.refs_7_), custom_call_target="tpu_custom_call" | custom-call | flops 2000000000 | tf_op jit(solution)/shard_map/second/pallas_call | solution.py:35
  14.7 3.5 %score.11.later.refs_0_ = f32[768,1152]{1,0:T(8,128)S(1)} custom-call(f32[1]{0:T(128)S(6)} %copy.33.log_scale.refs_0_, f32[1]{0:T(128)S(6)} %copy.34.bias.refs_1_, f32[768,1]{1,0:T(8,128)S(1)} %reshape.12.labels_x.refs_2_, bf16[784,1152]{1,0:T(8,128)(2,1)S(1)} %get-tuple-element.10.y.x.refs_3_, bf16[784,1152]{1,0:T(8,128)(2,1)S(1)} %get-tuple-element.11.x.y.value.refs_3_), custom_call_target="tpu_custom_call" | custom-call | flops 3500000000 | tf_op jit(solution)/shard_map/score/pallas_call | solution.py:35
  18.3 0.1 cut.3
  18.4 0.1 collective-permute-start.6
  18.5 0.9 collective-permute-start.2
  19.4 23.7 %collective-permute-done.raw = bf16[784,1152]{1,0:T(8,128)(2,1)S(1)} collective-permute-done((bf16[784,1152]{1,0:T(8,128)(2,1)S(1)}, bf16[784,1152]{1,0:T(8,128)(2,1)S(1)}, u32[]{:S(2)}, u32[]{:S(2)}) %collective-permute-start) | collective-permute-done | bytes 1806368 | tf_op jit(solution)/shard_map/ppermute | solution.py:306
  43.1 0.7 units.1.value.y
  43.8 0.1 collective-permute-start.1
  43.9 0.8 collective-permute-done.6.refs_4_
  44.7 6.3 %collective-permute-start.7 = (bf16[784,1152]{1,0:T(8,128)(2,1)S(1)}, bf16[784,1152]{1,0:T(8,128)(2,1)S(1)}, u32[]{:S(2)}, u32[]{:S(2)}) collective-permute-start(bf16[784,1152]{1,0:T(8,128)(2,1)S(1)} %collective-permute-done.6.refs_4_), channel_id=1, source_target_pairs={{0,1},{1,0},{2,3},{3,2},{4,5},{5,4},{6,7},{7,6},{8,9},{9,8},{10,11... | collective-permute-start | bytes 5419016 | tf_op jit(solution)/shard_map/ppermute | solution.py:306
  51.0 3.5 %score.8.refs_0_ = f32[768,1152]{1,0:T(8,128)S(1)} custom-call(f32[1]{0:T(128)S(6)} %copy.33.log_scale.refs_0_, f32[1]{0:T(128)S(6)} %copy.34.bias.refs_1_, f32[768,1]{1,0:T(8,128)S(1)} %reshape.12.labels_x.refs_2_, bf16[784,1152]{1,0:T(8,128)(2,1)S(1)} %get-tuple-element.11.x.y.value.refs_3_, bf16[784,1152]{1,0:T(8,128)(2,1)S(1)} %get-tuple-element.10.y.x.refs_3_), custom_call_target="tpu_custom_call" | custom-call | flops 3500000000 | tf_op jit(solution)/shard_map/score/pallas_call | solution.py:35
  54.5 0.0 collective-permute-done.2.y
  54.5 3.6 %score.9.refs_0_ = f32[768,1152]{1,0:T(8,128)S(1)} custom-call(f32[1]{0:T(128)S(6)} %copy.33.log_scale.refs_0_, f32[1]{0:T(128)S(6)} %copy.34.bias.refs_1_, f32[768,1]{1,0:T(8,128)S(1)} %reshape.12.labels_x.refs_2_, bf16[784,1152]{1,0:T(8,128)(2,1)S(1)} %get-tuple-element.11.x.y.value.refs_3_, ...), custom_call_target="tpu_custom_call", output_to_operand_aliasing={{}: (5, {})} | custom-call | flops 3500000000 | tf_op jit(solution)/shard_map/score/pallas_call | solution.py:35
  58.2 0.0 collective-permute-done.1.y
  58.2 3.8 %score.10.later.refs_5_ = f32[768,1152]{1,0:T(8,128)S(1)} custom-call(f32[1]{0:T(128)S(6)} %copy.33.log_scale.refs_0_, f32[1]{0:T(128)S(6)} %copy.34.bias.refs_1_, f32[768,1]{1,0:T(8,128)S(1)} %reshape.12.labels_x.refs_2_, bf16[784,1152]{1,0:T(8,128)(2,1)S(1)} %get-tuple-element.11.x.y.value.refs_3_, ...), custom_call_target="tpu_custom_call", output_to_operand_aliasing={{}: (5, {})} | custom-call | flops 3500000000 | tf_op jit(solution)/shard_map/score/pallas_call | solution.py:35
  61.9 0.1 cut.2
  62.1 0.1 collective-permute-start.4
  62.2 3.8 %score.12.refs_0_ = f32[768,1152]{1,0:T(8,128)S(1)} custom-call(f32[1]{0:T(128)S(6)} %copy.33.log_scale.refs_0_, f32[1]{0:T(128)S(6)} %copy.34.bias.refs_1_, f32[768,1]{1,0:T(8,128)S(1)} %reshape.12.labels_x.refs_2_, bf16[784,1152]{1,0:T(8,128)(2,1)S(1)} %get-tuple-element.10.y.x.refs_3_, ...), custom_call_target="tpu_custom_call", output_to_operand_aliasing={{}: (5, {})} | custom-call | flops 3500000000 | tf_op jit(solution)/shard_map/score/pallas_call | solution.py:35
  65.9 0.1 collective-permute-start.5
  66.0 0.3 collective-permute-start.3
  66.3 5.8 %finish.2 = (f32[768,1152]{1,0:T(8,128)}, f32[768,1152]{1,0:T(8,128)}) custom-call(f32[1]{0:T(128)S(6)} %copy.33.log_scale.refs_0_, f32[1]{0:T(128)S(6)} %copy.34.bias.refs_1_, f32[768,1]{1,0:T(8,128)S(1)} %reshape.12.labels_x.refs_2_, bf16[784,1152]{1,0:T(8,128)(2,1)S(1)} %get-tuple-element.11.x.y.value.refs_3_, ...), custom_call_target="tpu_custom_call" | custom-call | flops 5500000256 | tf_op jit(solution)/shard_map/finish/pallas_call | solution.py:35
  72.1 0.0 collective-permute-done.7.y
  72.1 3.7 %score.13.refs_0_ = f32[768,1152]{1,0:T(8,128)S(1)} custom-call(f32[1]{0:T(128)S(6)} %copy.33.log_scale.refs_0_, f32[1]{0:T(128)S(6)} %copy.34.bias.refs_1_, f32[768,1]{1,0:T(8,128)S(1)} %reshape.12.labels_x.refs_2_, bf16[784,1152]{1,0:T(8,128)(2,1)S(1)} %get-tuple-element.10.y.x.refs_3_, ...), custom_call_target="tpu_custom_call", output_to_operand_aliasing={{}: (5, {})} | custom-call | flops 3500000000 | tf_op jit(solution)/shard_map/score/pallas_call | solution.py:35
  75.8 5.5 %collective-permute-done.4.y.refs_0_.refs_5_ = bf16[400,1152]{1,0:T(8,128)(2,1)S(1)} collective-permute-done((bf16[400,1152]{1,0:T(8,128)(2,1)S(1)}, bf16[400,1152]{1,0:T(8,128)(2,1)S(1)}, u32[]{:S(2)}, u32[]{:S(2)}) %collective-permute-start.4) | collective-permute-done | bytes 921632 | tf_op jit(solution)/shard_map/ppermute | solution.py:306
  81.4 2.4 %score.14.refs_1_ = f32[768,1152]{1,0:T(8,128)S(1)} custom-call(f32[1]{0:T(128)S(6)} %copy.33.log_scale.refs_0_, f32[1]{0:T(128)S(6)} %copy.34.bias.refs_1_, f32[768,1]{1,0:T(8,128)S(1)} %reshape.12.labels_x.refs_2_, bf16[784,1152]{1,0:T(8,128)(2,1)S(1)} %get-tuple-element.10.y.x.refs_3_, ...), custom_call_target="tpu_custom_call", output_to_operand_aliasing={{}: (5, {})} | custom-call | flops 1750000000 | tf_op jit(solution)/shard_map/score/pallas_call | solution.py:35
  83.8 3.9 %collective-permute-done.5.y = bf16[256,1152]{1,0:T(8,128)(2,1)S(1)} collective-permute-done((bf16[256,1152]{1,0:T(8,128)(2,1)S(1)}, bf16[256,1152]{1,0:T(8,128)(2,1)S(1)}, u32[]{:S(2)}, u32[]{:S(2)}) %collective-permute-start.5) | collective-permute-done | bytes 589856 | tf_op jit(solution)/shard_map/ppermute | solution.py:306
  87.7 1.7 %score.15.refs_6_ = f32[768,1152]{1,0:T(8,128)S(1)} custom-call(f32[1]{0:T(128)S(6)} %copy.33.log_scale.refs_0_, f32[1]{0:T(128)S(6)} %copy.34.bias.refs_1_, f32[768,1]{1,0:T(8,128)S(1)} %reshape.12.labels_x.refs_2_, bf16[784,1152]{1,0:T(8,128)(2,1)S(1)} %get-tuple-element.10.y.x.refs_3_, ...), custom_call_target="tpu_custom_call", output_to_operand_aliasing={{}: (6, {})} | custom-call | flops 1166666624 | tf_op jit(solution)/shard_map/score/pallas_call | solution.py:35
  89.4 1.4 %collective-permute-done.3.refs_4_ = bf16[128,1152]{1,0:T(8,128)(2,1)S(1)} collective-permute-done((bf16[128,1152]{1,0:T(8,128)(2,1)S(1)}, bf16[128,1152]{1,0:T(8,128)(2,1)S(1)}, u32[]{:S(2)}, u32[]{:S(2)}) %collective-permute-start.3) | collective-permute-done | bytes 294944 | tf_op jit(solution)/shard_map/ppermute | solution.py:306
  90.8 3.5 %finish.3 = (f32[768,1152]{1,0:T(8,128)}, f32[768,1152]{1,0:T(8,128)}) custom-call(f32[1]{0:T(128)S(6)} %copy.33.log_scale.refs_0_, f32[1]{0:T(128)S(6)} %copy.34.bias.refs_1_, f32[768,1]{1,0:T(8,128)S(1)} %reshape.12.labels_x.refs_2_, bf16[784,1152]{1,0:T(8,128)(2,1)S(1)} %get-tuple-element.10.y.x.refs_3_, ...), custom_call_target="tpu_custom_call", output_to_operand_aliasing={{0}: (8, {}), {1}: (9, {})} | custom-call | flops 2583333376 | tf_op jit(solution)/shard_map/finish/pallas_call | solution.py:35
  (1 shorter events, 0.0 us)
Async XLA Ops:
  1.3 9.8 %copy-start = (s32[768]{0:T(1024)S(1)}, s32[768]{0:T(1024)}, u32[]{:S(2)}) copy-start(s32[768]{0:T(1024)} %param.7) | copy-start | bytes 9220
  2.8 40.4 %collective-permute-start = (bf16[784,1152]{1,0:T(8,128)(2,1)S(1)}, bf16[784,1152]{1,0:T(8,128)(2,1)S(1)}, u32[]{:S(2)}, u32[]{:S(2)}) collective-permute-start(bf16[784,1152]{1,0:T(8,128)(2,1)S(1)} %first.1.v_raw.refs_7_), channel_id=1, source_target_pairs={{0,127},{1,2},{2,1},{3,4},{4,3},{5,6},{6,5},{7,8},{8,7},{9,10},{10... | collective-permute-start | bytes 5419016 | tf_op jit(solution)/shard_map/ppermute | solution.py:306
  18.4 26.3 %collective-permute-start.6 = (bf16[784,1152]{1,0:T(8,128)(2,1)S(1)}, bf16[784,1152]{1,0:T(8,128)(2,1)S(1)}, u32[]{:S(2)}, u32[]{:S(2)}) collective-permute-start(bf16[784,1152]{1,0:T(8,128)(2,1)S(1)} %cut.3), channel_id=1, source_target_pairs={{0,3},{1,126},{2,5},{3,0},{4,7},{5,2},{6,9},{7,4},{8,11},{9,6},{10... | collective-permute-start | bytes 5419016 | tf_op jit(solution)/shard_map/ppermute | solution.py:306
  18.5 36.0 %collective-permute-start.2 = (bf16[784,1152]{1,0:T(8,128)(2,1)S(1)}, bf16[784,1152]{1,0:T(8,128)(2,1)S(1)}, u32[]{:S(2)}, u32[]{:S(2)}) collective-permute-start(bf16[784,1152]{1,0:T(8,128)(2,1)S(1)} %get-tuple-element.11.x.y.value.refs_3_), channel_id=1, source_target_pairs={{0,1},{1,0},{2,3},{3,2},{4,5},{5,4},{6,7},{7,6},{8,9},{9,8},{10,11... | collective-permute-start | bytes 5419016 | tf_op jit(solution)/shard_map/ppermute | solution.py:306
  43.8 14.3 %collective-permute-start.1 = (bf16[784,1152]{1,0:T(8,128)(2,1)S(1)}, bf16[784,1152]{1,0:T(8,128)(2,1)S(1)}, u32[]{:S(2)}, u32[]{:S(2)}) collective-permute-start(bf16[784,1152]{1,0:T(8,128)(2,1)S(1)} %units.1.value.y), channel_id=1, source_target_pairs={{0,1},{1,0},{2,3},{3,2},{4,5},{5,4},{6,7},{7,6},{8,9},{9,8},{10,11... | collective-permute-start | bytes 5419016 | tf_op jit(solution)/shard_map/ppermute | solution.py:306
  44.7 27.4 %collective-permute-start.7 = (bf16[784,1152]{1,0:T(8,128)(2,1)S(1)}, bf16[784,1152]{1,0:T(8,128)(2,1)S(1)}, u32[]{:S(2)}, u32[]{:S(2)}) collective-permute-start(bf16[784,1152]{1,0:T(8,128)(2,1)S(1)} %collective-permute-done.6.refs_4_), channel_id=1, source_target_pairs={{0,1},{1,0},{2,3},{3,2},{4,5},{5,4},{6,7},{7,6},{8,9},{9,8},{10,11... | collective-permute-start | bytes 5419016 | tf_op jit(solution)/shard_map/ppermute | solution.py:306
  62.1 19.3 %collective-permute-start.4 = (bf16[400,1152]{1,0:T(8,128)(2,1)S(1)}, bf16[400,1152]{1,0:T(8,128)(2,1)S(1)}, u32[]{:S(2)}, u32[]{:S(2)}) collective-permute-start(bf16[400,1152]{1,0:T(8,128)(2,1)S(1)} %get-tuple-element.13), channel_id=1, source_target_pairs={{0,2},{1,127},{2,4},{3,1},{4,6},{5,3},{6,8},{7,5},{8,10},{9,7},{10... | collective-permute-start | bytes 2764808 | tf_op jit(solution)/shard_map/ppermute | solution.py:306
  65.9 21.8 %collective-permute-start.5 = (bf16[256,1152]{1,0:T(8,128)(2,1)S(1)}, bf16[256,1152]{1,0:T(8,128)(2,1)S(1)}, u32[]{:S(2)}, u32[]{:S(2)}) collective-permute-start(bf16[256,1152]{1,0:T(8,128)(2,1)S(1)} %get-tuple-element.14), channel_id=1, source_target_pairs={{0,2},{1,127},{2,4},{3,1},{4,6},{5,3},{6,8},{7,5},{8,10},{9,7},{10... | collective-permute-start | bytes 1769480 | tf_op jit(solution)/shard_map/ppermute | solution.py:306
  66.0 24.8 %collective-permute-start.3 = (bf16[128,1152]{1,0:T(8,128)(2,1)S(1)}, bf16[128,1152]{1,0:T(8,128)(2,1)S(1)}, u32[]{:S(2)}, u32[]{:S(2)}) collective-permute-start(bf16[128,1152]{1,0:T(8,128)(2,1)S(1)} %get-tuple-element.12), channel_id=1, source_target_pairs={{0,2},{1,127},{2,4},{3,1},{4,6},{5,3},{6,8},{7,5},{8,10},{9,7},{10... | collective-permute-start | bytes 884744 | tf_op jit(solution)/shard_map/ppermute | solution.py:306

commit v3 on v2

--- a/solution.py
+++ b/solution.py
@@ -15,7 +15,6 @@
 PARTS = 4
 LIMIT = 16 * 1024 * 1024
 LOG2E = 1.4426950408889634
-MICROSECOND = 1.0e9
 ANY = pl.BlockSpec(memory_space=pl.ANY)
 HBM = pl.BlockSpec(memory_space=pltpu.HBM)
 VMEM = pl.BlockSpec(memory_space=pltpu.VMEM)
@@ -26,22 +25,39 @@
     return lax.rem(lax.axis_index(AXIS), 2) == 0
 
 
-def call(kernel, args, in_specs, out_shape, cost=1, **kw):
-    places = {id(VMEM): pltpu.VMEM, id(HBM): pltpu.HBM}
-    args = [
-        pltpu.with_memory_space_constraint(arg, places[id(spec)]) if id(spec) in places else arg
-        for arg, spec in zip(args, in_specs)
-    ]
-    return pl.pallas_call(
-        kernel,
-        out_shape=out_shape,
-        in_specs=in_specs,
-        compiler_params=pltpu.CompilerParams(vmem_limit_bytes=LIMIT),
-        cost_estimate=pl.CostEstimate(
-            flops=int(cost * MICROSECOND), bytes_accessed=0, transcendentals=0
-        ),
-        **kw,
-    )(*args)
+class Order:
+    def __init__(self):
+        self.token = None
+
+    def __call__(self, kernel, args, in_specs, out_shape, out_specs, scratch_shapes=(), **kw):
+        places = {id(VMEM): pltpu.VMEM, id(HBM): pltpu.HBM}
+        single = not isinstance(out_shape, list)
+        out_shape = [out_shape] if single else out_shape
+        out_specs = [out_specs] if single else out_specs
+        args = [
+            pltpu.with_memory_space_constraint(arg, places[id(spec)]) if id(spec) in places else arg
+            for arg, spec in zip(args, in_specs)
+        ]
+        n_in, n_out, first = len(args), len(out_shape), self.token is None
+        if not first:
+            args = [*args, self.token]
+            in_specs = [*in_specs, ANY]
+
+        def without_tokens(*refs):
+            rest = refs[len(args) :]
+            kernel(*refs[:n_in], *rest[:n_out], *rest[n_out + 1 :])
+
+        *outs, self.token = pl.pallas_call(
+            without_tokens,
+            out_shape=[*out_shape, pltpu.VMEM((8, 128), jnp.float32)],
+            in_specs=in_specs,
+            out_specs=[*out_specs, VMEM],
+            scratch_shapes=scratch_shapes,
+            compiler_params=pltpu.CompilerParams(vmem_limit_bytes=LIMIT),
+            cost_estimate=pl.CostEstimate(flops=int(20e9), bytes_accessed=0, transcendentals=0),
+            **kw,
+        )(*args)
+        return outs[0] if single else outs
 
 
 def inverse_norm(rows32):
@@ -96,7 +112,7 @@
     wait_pick(images, v_raw, sems)
 
 
-def first(images, texts, ids):
+def first(call, images, texts, ids):
     return call(
         first_kernel,
         [images, texts, ids],
@@ -116,7 +132,7 @@
     put_units(u_raw, u)
 
 
-def second(images, texts, ids, v_raw):
+def second(call, images, texts, ids, v_raw):
     return call(
         second_kernel,
         [images, texts, ids, v_raw],
@@ -125,11 +141,10 @@
         out_specs=[VMEM] * 3,
         scratch_shapes=[pltpu.SemaphoreType.DMA((PARTS,))],
         name="second",
-        cost=2,
-    )
-
-
-def units(raw):
+    )
+
+
+def units(call, raw):
     return call(
         put_units,
         [raw],
@@ -137,11 +152,10 @@
         pltpu.VMEM(raw.shape, raw.dtype),
         out_specs=VMEM,
         name="units",
-        cost=0.7,
-    )
-
-
-def cut_kernel(value, later, *outs):
+    )
+
+
+def cut_kernel(value, *outs):
     start = 0
     for out in outs:
         size = out.shape[0] if len(outs) == 1 or start else out.shape[0] - LABEL_ROWS
@@ -151,15 +165,14 @@
         start += size
 
 
-def cut(value, later, sizes):
+def cut(call, value, sizes):
     return call(
         cut_kernel,
-        [value, later],
-        [VMEM, ANY],
+        [value],
+        [VMEM],
         [pltpu.VMEM((size, value.shape[1]), value.dtype) for size in sizes],
         out_specs=[VMEM] * len(sizes),
         name="cut",
-        cost=0.2,
     )
 
 
@@ -205,12 +218,11 @@
     size = y.shape[0] if labelled is not None else labels_at
     args = [*scalars, labels_x, x, y] + ([labelled] if labelled is not None else [])
     in_specs = [SMEM, SMEM] + [VMEM] * (len(args) - 2)
-    cost = 3.5 * size / ROWS
-    return args, in_specs, (labels_at, start, size), cost
-
-
-def score(scalars, labels_x, x, y, before=None, labelled=None, labels_at=ROWS, start=0):
-    args, in_specs, where, cost = score_args(
+    return args, in_specs, (labels_at, start, size)
+
+
+def score(call, scalars, labels_x, x, y, before=None, labelled=None, labels_at=ROWS, start=0):
+    args, in_specs, where = score_args(
         scalars, labels_x, x, y, labelled, labels_at, start
     )
     aliases = {}
@@ -226,7 +238,6 @@
         out_specs=VMEM,
         input_output_aliases=aliases,
         name="score",
-        cost=cost,
     )
 
 
@@ -261,6 +272,7 @@
 
 
 def finish(
+    call,
     scalars,
     labels_x,
     x,
@@ -273,7 +285,7 @@
     labels_at=ROWS,
     start=0,
 ):
-    args, in_specs, where, cost = score_args(
+    args, in_specs, where = score_args(
         scalars, labels_x, x, y, labelled, labels_at, start
     )
     args += [before, raw]
@@ -296,7 +308,6 @@
             pltpu.SemaphoreType.DMA((ROWS // TILE,)),
         ],
         name="finish",
-        cost=cost + 2,
     )
 
 
@@ -311,40 +322,42 @@
 
 
 def on_device(images, texts, pair_ids, log_scale, bias):
+    call = Order()
     scalars = (log_scale, bias)
     ids = pair_ids.reshape(1, ROWS)
     labels = pair_ids.astype(jnp.float32).reshape(ROWS, 1)
 
-    v_raw = first(images, texts, ids)
+    v_raw = first(call, images, texts, ids)
     x_raw = permute(v_raw, -1, 1)
-    u_raw, u, v = second(images, texts, ids, v_raw)
+    u_raw, u, v = second(call, images, texts, ids, v_raw)
     s0 = swap(u)
-    grad_u = score(scalars, labels, u, v)
-    grad_v = score(scalars, labels, v, u)
-    (u_again,) = cut(u, grad_v, (u.shape[0],))
+    grad_u = score(call, scalars, labels, u, v)
+    grad_v = score(call, scalars, labels, v, u)
+    (u_again,) = cut(call, u, (u.shape[0],))
     y = permute(u_again, 3, -3)
-    grad_u = score(scalars, labels, u, s0, grad_u)
-
-    x = units(x_raw)
+    grad_u = score(call, scalars, labels, u, s0, grad_u)
+
+    x = units(call, x_raw)
     s1 = swap(x)
-    grad_v = score(scalars, labels, v, x, grad_v)
-    grad_u = score(scalars, labels, u, s1, grad_u)
+    grad_v = score(call, scalars, labels, v, x, grad_v)
     sizes = (PIECES[0] + LABEL_ROWS, *PIECES[1:])
-    z = [permute(piece, 2, -2) for piece in cut(x, grad_u, sizes)]
-
-    s2 = swap(y)
-    outs = finish(scalars, labels, u, y, grad_u, u_raw, True)
-    grad_v = score(scalars, labels, v, s2, grad_v)
-
-    grad_v = score(scalars, labels, v, z[0], grad_v, labels_at=PIECES[0])
+    z = [permute(piece, 2, -2) for piece in cut(call, x, sizes)]
+    grad_u = score(call, scalars, labels, u, s1, grad_u)
+
+    (y_again,) = cut(call, y, (y.shape[0],))
+    s2 = swap(y_again)
+    outs = finish(call, scalars, labels, u, y, grad_u, u_raw, True)
+    grad_v = score(call, scalars, labels, v, s2, grad_v)
+
+    grad_v = score(call, scalars, labels, v, z[0], grad_v, labels_at=PIECES[0])
     start = PIECES[0]
     for piece in z[1:]:
         place = dict(labelled=z[0], labels_at=PIECES[0], start=start)
         start += piece.shape[0]
         if start < ROWS:
-            grad_v = score(scalars, labels, v, piece, grad_v, **place)
+            grad_v = score(call, scalars, labels, v, piece, grad_v, **place)
         else:
-            outs = finish(scalars, labels, v, piece, grad_v, v_raw, False, outs, **place)
+            outs = finish(call, scalars, labels, v, piece, grad_v, v_raw, False, outs, **place)
     return tuple(outs)
 
 

time: 94.8 us -> 79 us (0.83)
  waiting for transfers between devices: 35.3 us -> 18.1 us
    ppermute x8, waiting for transfers between devices: 35.3 us -> 18.1 us  [permute(): return lax.ppermute(value, AXIS, pairs)]
    pallas_call x15 -> x16, Pallas kernels: 39.9 us -> 40.5 us  [__call__(): pl.pallas_call(without_tokens, out_shape=[*out_shape, pltpu.VMEM((8, 128)...]
  transfers between devices with their start and end apart: 8 -> 8, of which waited for: 5 -> 3; matrix products, arithmetic and copies ran while one was open for 0% -> 0% of each run, Pallas kernels for 37% -> 44%
where the time goes in v3:
time: 79 us; the launch traced here: 78.7 us
  Pallas kernels  40.5 us (51%)
  waiting for transfers between devices  18.1 us (23%)
  starting transfers between devices  17 us (22%)
  between operations  2.34 us (3%)
  local copies, waits for them, and re-layouts  0.86 us (1%)
    pallas_call x16, Pallas kernels, __call__(): pl.pallas_call(without_tokens, out_shape=[*out_shape, pltpu.VMEM((8, 128)...  40.5 us
    ppermute x8, waiting for transfers between devices, permute(): return lax.ppermute(value, AXIS, pairs)  18.1 us
    ppermute x8, starting transfers between devices, permute(): return lax.ppermute(value, AXIS, pairs)  17 us
  transfers between devices with their start and end apart: 8, of which 3 were waited for; matrix products, arithmetic and copies ran while one was open for 0% of the time, Pallas kernels for 44%

profile of v3, /device:TPU:0, one launch (start us, length us, event | category | flops | bytes accessed | tf_op | source)
XLA Modules:
  0.0 78.7 jit_solution(16263401347313058996)
XLA Ops:
  0.6 0.7 reshape.11.refs_2_
  1.3 1.5 %first.1 = (bf16[784,1152]{1,0:T(8,128)(2,1)S(1)}, f32[8,128]{1,0:T(8,128)S(1)}) custom-call(bf16[768,1152]{1,0:T(8,128)(2,1)} %refs_0_.13, bf16[768,1152]{1,0:T(8,128)(2,1)} %refs_1_.13, s32[1,768]{1,0:T(1,128)S(1)} %reshape.11.refs_2_), custom_call_target="tpu_custom_call" | custom-call | flops 20000000000 | tf_op jit(solution)/shard_map/first/pallas_call | solution.py:50
  2.8 0.0 copy-start
  2.8 8.3 %collective-permute-start = (bf16[784,1152]{1,0:T(8,128)(2,1)S(1)}, bf16[784,1152]{1,0:T(8,128)(2,1)S(1)}, u32[]{:S(2)}, u32[]{:S(2)}) collective-permute-start(bf16[784,1152]{1,0:T(8,128)(2,1)S(1)} %get-tuple-element.39.refs_3_.refs_7_), channel_id=1, source_target_pairs={{0,127},{1,2},{2,1},{3,4},{4,3},{5,6},{6,5},{7,8},{8,7},{9,10},{10... | collective-permute-start | bytes 5419016 | tf_op jit(solution)/shard_map/ppermute | solution.py:317
  11.1 0.0 copy-start.2
  11.1 2.1 %second.1 = (bf16[784,1152]{1,0:T(8,128)(2,1)S(1)}, bf16[784,1152]{1,0:T(8,128)(2,1)S(1)}, bf16[784,1152]{1,0:T(8,128)(2,1)S(1)}, f32[8,128]{1,0:T(8,128)S(1)}) custom-call(bf16[768,1152]{1,0:T(8,128)(2,1)} %refs_0_.13, bf16[768,1152]{1,0:T(8,128)(2,1)} %refs_1_.13, s32[1,768]{1,0:T(1,128)S(1)} %reshape.11.refs_2_, ...), custom_call_target="tpu_custom_call" | custom-call | flops 20000000000 | tf_op jit(solution)/shard_map/second/pallas_call | solution.py:50
  13.2 0.0 copy-done
  13.2 0.1 collective-permute-start.1
  13.3 0.0 copy-done.2
  14.6 0.2 reshape.12.refs_2_
  14.8 3.5 %score.8 = (f32[768,1152]{1,0:T(8,128)S(1)}, f32[8,128]{1,0:T(8,128)S(1)}) custom-call(f32[1]{0:T(128)S(6)} %copy.33.refs_0_, f32[1]{0:T(128)S(6)} %copy.34.refs_1_, f32[768,1]{1,0:T(8,128)S(1)} %reshape.12.refs_2_, bf16[784,1152]{1,0:T(8,128)(2,1)S(1)} %get-tuple-element.42.refs_3_.refs_4_.refs_0_, bf16[784,1152]{1,0:T(8,128)(2,1)S(1)} %get-tuple-element.41.refs_4_.refs_3_, ...), custom_call_target="tpu_custom_call" | custom-call | flops 20000000000 | tf_op jit(solution)/shard_map/score/pallas_call | solution.py:50
  18.3 3.5 %score.9 = (f32[768,1152]{1,0:T(8,128)S(1)}, f32[8,128]{1,0:T(8,128)S(1)}) custom-call(f32[1]{0:T(128)S(6)} %copy.33.refs_0_, f32[1]{0:T(128)S(6)} %copy.34.refs_1_, f32[768,1]{1,0:T(8,128)S(1)} %reshape.12.refs_2_, bf16[784,1152]{1,0:T(8,128)(2,1)S(1)} %get-tuple-element.41.refs_4_.refs_3_, bf16[784,1152]{1,0:T(8,128)(2,1)S(1)} %get-tuple-element.42.refs_3_.refs_4_.refs_0_, ...), custom_call_target="tpu_custom_call" | custom-call | flops 20000000000 | tf_op jit(solution)/shard_map/score/pallas_call | solution.py:50
  21.9 0.1 cut.3
  22.0 0.3 collective-permute-start.5
  22.3 0.0 collective-permute-done.1.refs_4_
  22.3 3.6 %score.10 = (f32[768,1152]{1,0:T(8,128)S(1)}, f32[8,128]{1,0:T(8,128)S(1)}) custom-call(f32[1]{0:T(128)S(6)} %copy.33.refs_0_, f32[1]{0:T(128)S(6)} %copy.34.refs_1_, f32[768,1]{1,0:T(8,128)S(1)} %reshape.12.refs_2_, bf16[784,1152]{1,0:T(8,128)(2,1)S(1)} %get-tuple-element.42.refs_3_.refs_4_.refs_0_, ...), custom_call_target="tpu_custom_call", output_to_operand_aliasing={{0}: (5, {})} | custom-call | flops 20000000000 | tf_op jit(solution)/shard_map/score/pallas_call | solution.py:50
  25.9 13.1 %collective-permute-done.refs_0_ = bf16[784,1152]{1,0:T(8,128)(2,1)S(1)} collective-permute-done((bf16[784,1152]{1,0:T(8,128)(2,1)S(1)}, bf16[784,1152]{1,0:T(8,128)(2,1)S(1)}, u32[]{:S(2)}, u32[]{:S(2)}) %collective-permute-start) | collective-permute-done | bytes 1806368 | tf_op jit(solution)/shard_map/ppermute | solution.py:317
  39.1 0.7 units.1
  39.7 0.1 collective-permute-start.6
  39.8 3.7 %score.11 = (f32[768,1152]{1,0:T(8,128)S(1)}, f32[8,128]{1,0:T(8,128)S(1)}) custom-call(f32[1]{0:T(128)S(6)} %copy.33.refs_0_, f32[1]{0:T(128)S(6)} %copy.34.refs_1_, f32[768,1]{1,0:T(8,128)S(1)} %reshape.12.refs_2_, bf16[784,1152]{1,0:T(8,128)(2,1)S(1)} %get-tuple-element.41.refs_4_.refs_3_, ...), custom_call_target="tpu_custom_call", output_to_operand_aliasing={{0}: (5, {})} | custom-call | flops 20000000000 | tf_op jit(solution)/shard_map/score/pallas_call | solution.py:50
  43.6 0.1 cut.4
  43.7 0.1 collective-permute-start.2
  43.8 0.1 collective-permute-start.3
  43.9 0.1 collective-permute-start.4
  44.0 0.0 collective-permute-done.6.refs_4_
  44.0 3.6 %score.12 = (f32[768,1152]{1,0:T(8,128)S(1)}, f32[8,128]{1,0:T(8,128)S(1)}) custom-call(f32[1]{0:T(128)S(6)} %copy.33.refs_0_, f32[1]{0:T(128)S(6)} %copy.34.refs_1_, f32[768,1]{1,0:T(8,128)S(1)} %reshape.12.refs_2_, bf16[784,1152]{1,0:T(8,128)(2,1)S(1)} %get-tuple-element.42.refs_3_.refs_4_.refs_0_, ...), custom_call_target="tpu_custom_call", output_to_operand_aliasing={{0}: (5, {})} | custom-call | flops 20000000000 | tf_op jit(solution)/shard_map/score/pallas_call | solution.py:50
  47.6 0.0 collective-permute-done.5.refs_0_.refs_4_
  47.6 0.1 cut.5
  47.8 8.0 %collective-permute-start.7 = (bf16[784,1152]{1,0:T(8,128)(2,1)S(1)}, bf16[784,1152]{1,0:T(8,128)(2,1)S(1)}, u32[]{:S(2)}, u32[]{:S(2)}) collective-permute-start(bf16[784,1152]{1,0:T(8,128)(2,1)S(1)} %get-tuple-element.60), channel_id=1, source_target_pairs={{0,1},{1,0},{2,3},{3,2},{4,5},{5,4},{6,7},{7,6},{8,9},{9,8},{10,11... | collective-permute-start | bytes 5419016 | tf_op jit(solution)/shard_map/ppermute | solution.py:317
  55.8 5.8 %finish.2 = (f32[768,1152]{1,0:T(8,128)}, f32[768,1152]{1,0:T(8,128)}, f32[8,128]{1,0:T(8,128)S(1)}) custom-call(f32[1]{0:T(128)S(6)} %copy.33.refs_0_, f32[1]{0:T(128)S(6)} %copy.34.refs_1_, f32[768,1]{1,0:T(8,128)S(1)} %reshape.12.refs_2_, bf16[784,1152]{1,0:T(8,128)(2,1)S(1)} %get-tuple-element.42.refs_3_.refs_4_.refs_0_, ...), custom_call_target="tpu_custom_call" | custom-call | flops 20000000000 | tf_op jit(solution)/shard_map/finish/pallas_call | solution.py:50
  61.6 0.0 collective-permute-done.7.refs_4_
  61.6 3.7 %score.13 = (f32[768,1152]{1,0:T(8,128)S(1)}, f32[8,128]{1,0:T(8,128)S(1)}) custom-call(f32[1]{0:T(128)S(6)} %copy.33.refs_0_, f32[1]{0:T(128)S(6)} %copy.34.refs_1_, f32[768,1]{1,0:T(8,128)S(1)} %reshape.12.refs_2_, bf16[784,1152]{1,0:T(8,128)(2,1)S(1)} %get-tuple-element.41.refs_4_.refs_3_, ...), custom_call_target="tpu_custom_call", output_to_operand_aliasing={{0}: (5, {})} | custom-call | flops 20000000000 | tf_op jit(solution)/shard_map/score/pallas_call | solution.py:50
  65.3 1.1 %collective-permute-done.3.refs_4_.refs_5_ = bf16[400,1152]{1,0:T(8,128)(2,1)S(1)} collective-permute-done((bf16[400,1152]{1,0:T(8,128)(2,1)S(1)}, bf16[400,1152]{1,0:T(8,128)(2,1)S(1)}, u32[]{:S(2)}, u32[]{:S(2)}) %collective-permute-start.3) | collective-permute-done | bytes 921632 | tf_op jit(solution)/shard_map/ppermute | solution.py:317
  66.4 2.4 %score.14 = (f32[768,1152]{1,0:T(8,128)S(1)}, f32[8,128]{1,0:T(8,128)S(1)}) custom-call(f32[1]{0:T(128)S(6)} %copy.33.refs_0_, f32[1]{0:T(128)S(6)} %copy.34.refs_1_, f32[768,1]{1,0:T(8,128)S(1)} %reshape.12.refs_2_, bf16[784,1152]{1,0:T(8,128)(2,1)S(1)} %get-tuple-element.41.refs_4_.refs_3_, ...), custom_call_target="tpu_custom_call", output_to_operand_aliasing={{0}: (5, {})} | custom-call | flops 20000000000 | tf_op jit(solution)/shard_map/score/pallas_call | solution.py:50
  68.8 3.9 %collective-permute-done.4.refs_4_ = bf16[256,1152]{1,0:T(8,128)(2,1)S(1)} collective-permute-done((bf16[256,1152]{1,0:T(8,128)(2,1)S(1)}, bf16[256,1152]{1,0:T(8,128)(2,1)S(1)}, u32[]{:S(2)}, u32[]{:S(2)}) %collective-permute-start.4) | collective-permute-done | bytes 589856 | tf_op jit(solution)/shard_map/ppermute | solution.py:317
  72.7 0.0 copy-start.1
  72.7 1.7 %score.15 = (f32[768,1152]{1,0:T(8,128)S(1)}, f32[8,128]{1,0:T(8,128)S(1)}) custom-call(f32[1]{0:T(128)S(6)} %copy.33.refs_0_, f32[1]{0:T(128)S(6)} %copy.34.refs_1_, f32[768,1]{1,0:T(8,128)S(1)} %reshape.12.refs_2_, bf16[784,1152]{1,0:T(8,128)(2,1)S(1)} %get-tuple-element.41.refs_4_.refs_3_, ...), custom_call_target="tpu_custom_call", output_to_operand_aliasing={{0}: (6, {})} | custom-call | flops 20000000000 | tf_op jit(solution)/shard_map/score/pallas_call | solution.py:50
  74.4 0.0 collective-permute-done.2.refs_4_
  74.4 0.0 copy-done.1
  74.4 4.1 %finish.3 = (f32[768,1152]{1,0:T(8,128)}, f32[768,1152]{1,0:T(8,128)}, f32[8,128]{1,0:T(8,128)}) custom-call(f32[1]{0:T(128)S(6)} %copy.33.refs_0_, f32[1]{0:T(128)S(6)} %copy.34.refs_1_, f32[768,1]{1,0:T(8,128)S(1)} %reshape.12.refs_2_, bf16[784,1152]{1,0:T(8,128)(2,1)S(1)} %get-tuple-element.41.refs_4_.refs_3_, ...), custom_call_target="tpu_custom_call", output_to_operand_aliasing={{0}: (8, {}), {1}: (9, {})} | custom-call | flops 20000000000 | tf_op jit(solution)/shard_map/finish/pallas_call | solution.py:50
  (1 shorter events, 0.0 us)
Async XLA Ops:
  2.8 10.4 %copy-start = (bf16[784,1152]{1,0:T(8,128)(2,1)}, bf16[784,1152]{1,0:T(8,128)(2,1)S(1)}, u32[]{:S(2)}) copy-start(bf16[784,1152]{1,0:T(8,128)(2,1)S(1)} %get-tuple-element.39.refs_3_.refs_7_) | copy-start | bytes 5419012
  2.8 36.3 %collective-permute-start = (bf16[784,1152]{1,0:T(8,128)(2,1)S(1)}, bf16[784,1152]{1,0:T(8,128)(2,1)S(1)}, u32[]{:S(2)}, u32[]{:S(2)}) collective-permute-start(bf16[784,1152]{1,0:T(8,128)(2,1)S(1)} %get-tuple-element.39.refs_3_.refs_7_), channel_id=1, source_target_pairs={{0,127},{1,2},{2,1},{3,4},{4,3},{5,6},{6,5},{7,8},{8,7},{9,10},{10... | collective-permute-start | bytes 5419016 | tf_op jit(solution)/shard_map/ppermute | solution.py:317
  11.1 2.2 %copy-start.2 = (s32[768]{0:T(1024)S(1)}, s32[768]{0:T(1024)}, u32[]{:S(2)}) copy-start(s32[768]{0:T(1024)} %param.7) | copy-start | bytes 9220
  13.2 9.1 %collective-permute-start.1 = (bf16[784,1152]{1,0:T(8,128)(2,1)S(1)}, bf16[784,1152]{1,0:T(8,128)(2,1)S(1)}, u32[]{:S(2)}, u32[]{:S(2)}) collective-permute-start(bf16[784,1152]{1,0:T(8,128)(2,1)S(1)} %get-tuple-element.42.refs_3_.refs_4_.refs_0_), channel_id=1, source_target_pairs={{0,1},{1,0},{2,3},{3,2},{4,5},{5,4},{6,7},{7,6},{8,9},{9,8},{10,11... | collective-permute-start | bytes 5419016 | tf_op jit(solution)/shard_map/ppermute | solution.py:317
  22.0 25.6 %collective-permute-start.5 = (bf16[784,1152]{1,0:T(8,128)(2,1)S(1)}, bf16[784,1152]{1,0:T(8,128)(2,1)S(1)}, u32[]{:S(2)}, u32[]{:S(2)}) collective-permute-start(bf16[784,1152]{1,0:T(8,128)(2,1)S(1)} %get-tuple-element.56), channel_id=1, source_target_pairs={{0,3},{1,126},{2,5},{3,0},{4,7},{5,2},{6,9},{7,4},{8,11},{9,6},{10... | collective-permute-start | bytes 5419016 | tf_op jit(solution)/shard_map/ppermute | solution.py:317
  39.7 4.2 %collective-permute-start.6 = (bf16[784,1152]{1,0:T(8,128)(2,1)S(1)}, bf16[784,1152]{1,0:T(8,128)(2,1)S(1)}, u32[]{:S(2)}, u32[]{:S(2)}) collective-permute-start(bf16[784,1152]{1,0:T(8,128)(2,1)S(1)} %get-tuple-element.49.refs_4_.refs_0_), channel_id=1, source_target_pairs={{0,1},{1,0},{2,3},{3,2},{4,5},{5,4},{6,7},{7,6},{8,9},{9,8},{10,11... | collective-permute-start | bytes 5419016 | tf_op jit(solution)/shard_map/ppermute | solution.py:317
  43.7 30.7 %collective-permute-start.2 = (bf16[128,1152]{1,0:T(8,128)(2,1)S(1)}, bf16[128,1152]{1,0:T(8,128)(2,1)S(1)}, u32[]{:S(2)}, u32[]{:S(2)}) collective-permute-start(bf16[128,1152]{1,0:T(8,128)(2,1)S(1)} %get-tuple-element.53), channel_id=1, source_target_pairs={{0,2},{1,127},{2,4},{3,1},{4,6},{5,3},{6,8},{7,5},{8,10},{9,7},{10... | collective-permute-start | bytes 884744 | tf_op jit(solution)/shard_map/ppermute | solution.py:317
  43.8 22.6 %collective-permute-start.3 = (bf16[400,1152]{1,0:T(8,128)(2,1)S(1)}, bf16[400,1152]{1,0:T(8,128)(2,1)S(1)}, u32[]{:S(2)}, u32[]{:S(2)}) collective-permute-start(bf16[400,1152]{1,0:T(8,128)(2,1)S(1)} %get-tuple-element.54), channel_id=1, source_target_pairs={{0,2},{1,127},{2,4},{3,1},{4,6},{5,3},{6,8},{7,5},{8,10},{9,7},{10... | collective-permute-start | bytes 2764808 | tf_op jit(solution)/shard_map/ppermute | solution.py:317
  43.9 28.8 %collective-permute-start.4 = (bf16[256,1152]{1,0:T(8,128)(2,1)S(1)}, bf16[256,1152]{1,0:T(8,128)(2,1)S(1)}, u32[]{:S(2)}, u32[]{:S(2)}) collective-permute-start(bf16[256,1152]{1,0:T(8,128)(2,1)S(1)} %get-tuple-element.55), channel_id=1, source_target_pairs={{0,2},{1,127},{2,4},{3,1},{4,6},{5,3},{6,8},{7,5},{8,10},{9,7},{10... | collective-permute-start | bytes 1769480 | tf_op jit(solution)/shard_map/ppermute | solution.py:317
  47.8 13.8 %collective-permute-start.7 = (bf16[784,1152]{1,0:T(8,128)(2,1)S(1)}, bf16[784,1152]{1,0:T(8,128)(2,1)S(1)}, u32[]{:S(2)}, u32[]{:S(2)}) collective-permute-start(bf16[784,1152]{1,0:T(8,128)(2,1)S(1)} %get-tuple-element.60), channel_id=1, source_target_pairs={{0,1},{1,0},{2,3},{3,2},{4,5},{5,4},{6,7},{7,6},{8,9},{9,8},{10,11... | collective-permute-start | bytes 5419016 | tf_op jit(solution)/shard_map/ppermute | solution.py:317
  72.7 1.7 %copy-start.1 = (bf16[784,1152]{1,0:T(8,128)(2,1)S(1)}, bf16[784,1152]{1,0:T(8,128)(2,1)}, u32[]{:S(2)}) copy-start(bf16[784,1152]{1,0:T(8,128)(2,1)} %copy-done) | copy-start | bytes 5419012
